TPU v7x, 256 devices: a whole 4x4x8 slice. The times are simulated.
256 devices in a mesh: row: 8 (over z_hi, x), col: 32 (over z_lo, y, core).
Axes of the slice: x: 4, y: 4, z: 8 (z_hi: 2, z_lo: 4; z = z_hi * 4 + z_lo), core: 2. Of those that a mesh axis runs over, the one named last changes fastest.
Arguments:
- lower_panel: float32 [3, 16384, 256], P(None, ('row', 'col')), may hold values from -6 to 6
- panel_mask: int32 [3, 128], P(None, 'row'), may hold values 0 or 1
- inverse_tiles: float32 [3, 16384, 16384], P(None, 'col', 'row'), may hold values from -0.125 to 0.125
- tile_mask: int32 [3, 128, 128], P(None, 'col', 'row'), may hold values from 0 to 1, as said below
Outputs:
- inverse_panel: float32 [3, 16384, 256], P(None, ('col', 'row'))
Inputs may be any that keep to these rules, and one draw needn't show every extreme that they name: `tile_mask`: 1 marks a present block, 0 an absent one; the share of present blocks differs from block row to block row.
All inputs are finite; a program needn't handle non-finite values. No bound on the sum of `panel_mask` on one device may be relied on, other than what follows from the above.
Results may differ from a plain program's by a relative error of at most 0.00007.
Values sent between devices are 32-bit elements; how exact they have to be, the bound alone decides.
No kernel may reach another device: no remote copies, remote signals or barrier semaphores. Data moves between devices by JAX's collectives and lax.ppermute only.
A program may use at most 128 MiB of HBM per device.

v0:
```python
import functools

import jax
import jax.numpy as jnp
from jax import lax
from jax.experimental import pallas as pl
from jax.experimental.pallas import tpu as pltpu
from jax.sharding import Mesh
from jax.sharding import PartitionSpec as P

AXES = ("zh", "x", "zl", "y", "core")
SIZES = (2, 4, 4, 4, 2)
BLK = 128
MIB = 1 << 20


def swap(value, axis, by, name):
    pairs = [(2 * i + core, 2 * (i ^ by[core]) + core) for i in range(SIZES[AXES.index(axis)]) for core in range(2)]
    with jax.named_scope(name):
        return lax.ppermute(value, (axis, "core"), pairs)


def swap_core(value, name):
    with jax.named_scope(name):
        return lax.ppermute(value, "core", [(0, 1), (1, 0)])


def split(value):
    high = value.astype(jnp.bfloat16)
    low = (value - high.astype(jnp.float32)).astype(jnp.bfloat16)
    return high, low


def ring_order(core):
    return [0, 1 + 2 * core, 3 - 2 * core, 2]


def tiles_kernel(spot, factors, tiles, high, low, held, arrived):
    zh, x, core = spot[0], spot[1], spot[4]
    own, first, second, both = ring_order(core)
    sources = [(zh ^ dz) * 4 + (x ^ dx) for dx in (own, second, first, both) for dz in range(2)]
    number, height, _ = tiles.shape
    rows = height // len(sources)

    def copy(n, i):
        rows_from = pl.ds(pl.multiple_of(sources[i] * rows, rows), rows)
        return pltpu.make_async_copy(tiles.at[n, rows_from], held.at[n, pl.ds(i * rows, rows)], arrived.at[n, i])

    @pl.loop(0, number)
    def _(n):
        for i in range(len(sources)):
            copy(n, i).start()

    @pl.loop(0, number)
    def _(n):
        for i, source in enumerate(sources):
            copy(n, i).wait()
            to = pl.ds(i * rows, rows)
            high[n, to], low[n, to] = split(held[n, to] * factors[n, source // 2])


def split_tiles(spot, tiles, factors):
    out = jax.ShapeDtypeStruct(tiles.shape, jnp.bfloat16)
    whole = pl.BlockSpec(memory_space=pltpu.VMEM)
    return pl.pallas_call(
        tiles_kernel,
        out_shape=[out, out],
        in_specs=[pl.BlockSpec(memory_space=pltpu.SMEM), whole, pl.BlockSpec(memory_space=pltpu.HBM)],
        out_specs=[whole, whole],
        scratch_shapes=[pltpu.VMEM(tiles.shape, jnp.float32), pltpu.SemaphoreType.DMA((tiles.shape[0], 8))],
        compiler_params=pltpu.CompilerParams(vmem_limit_bytes=40 * MIB),
        name="split_tiles",
    )(spot, factors, tiles)


def product_kernel(n, spot, high, low, near, far, near_other, far_other, keep, send, panel_high, panel_low):
    zl, y, core = spot[2], spot[3], spot[4]
    for dc, pieces in enumerate(((near, far), (near_other, far_other))):
        order = ring_order(core ^ dc)
        for piece, dys in zip(pieces, (order[:2], order[2:])):
            for part, (dy, dz) in enumerate((dy, dz) for dy in dys for dz in (0, 2, 1, 3)):
                block = ((zl ^ dz) * 4 + (y ^ dy)) * 2 + (core ^ dc)
                rows = pl.ds(pl.multiple_of(block * 64, 64), 64)
                panel_high[rows, :], panel_low[rows, :] = split(piece[pl.ds(part * 64, 64), :])
    dot = functools.partial(jnp.dot, preferred_element_type=jnp.float32)
    step = high.shape[1] // 2
    for half, out in enumerate((keep, send)):
        rows = pl.ds(half * step, step)
        total = dot(low[0, rows, :], panel_high[...])
        total += dot(high[0, rows, :], panel_low[...])
        total += dot(high[0, rows, :], panel_high[...])
        out[...] = total


def product(n, spot, high, low, pieces):
    height, breadth = high.shape[1:]
    width = pieces[0].shape[1]
    whole = pl.BlockSpec(memory_space=pltpu.VMEM)
    tile_spec = pl.BlockSpec((1, height, breadth), lambda i: (n, 0, 0))
    return pl.pallas_call(
        functools.partial(product_kernel, n),
        out_shape=[jax.ShapeDtypeStruct((height // 2, width), jnp.float32)] * 2,
        grid=(1,),
        in_specs=[pl.BlockSpec(memory_space=pltpu.SMEM), tile_spec, tile_spec] + [whole] * len(pieces),
        out_specs=[whole] * 2,
        scratch_shapes=[pltpu.VMEM((breadth, width), jnp.bfloat16)] * 2,
        compiler_params=pltpu.CompilerParams(vmem_limit_bytes=20 * MIB),
        name="product",
    )(spot, high, low, *pieces)


def local(lower_panel, panel_mask, inverse_tiles, tile_mask):
    number = lower_panel.shape[0]
    spot = jnp.stack([lax.axis_index(a) for a in AXES]).astype(jnp.int32)
    factors = -(tile_mask * panel_mask[:, None, :]).astype(jnp.float32)
    factors = jnp.repeat(factors, BLK, axis=2)[:, :, None, :]
    def after(value, *gates):
        return lax.optimization_barrier((value, gates))[0]

    def grow(value, axis, by, name):
        return jnp.concatenate([value, swap(value, axis, by, name)], axis=-2)

    def halves(total):
        half = total.shape[0] // 2
        return total[:half], total[half:]

    def add_half(keep, send, axis, by, name):
        return keep + swap(send, axis, by, name)

    near_z, far_z, first, second, across = (1, 1), (2, 2), (1, 3), (3, 1), (1, 1)

    a0 = grow(lower_panel[0], "zl", far_z, "z_far_0")
    a12 = grow(lower_panel[1:], "zl", far_z, "z_far_12")
    g0 = grow(a0, "zl", near_z, "z_near_0")
    g12 = grow(a12, "zl", near_z, "z_near_12")
    n0 = grow(g0, "y", first, "y_first_0")
    high, low = split_tiles(spot, inverse_tiles, after(factors, n0))
    f0 = swap(n0, "y", second, "y_second_0")
    n12 = grow(after(g12, n0), "y", first, "y_first_12")
    outs0 = product(0, spot, high, low, [n0, f0, swap_core(n0, "core_near_0"), swap_core(after(f0, high), "core_far_0")])
    n1, n2 = n12[0], n12[1]
    f1 = swap(n1, "y", second, "y_second_1")
    f2 = swap(n2, "y", second, "y_second_2")
    x0 = add_half(*outs0, "x", first, "x_first_0")
    c1 = [swap_core(n1, "core_near_1"), swap_core(after(f1, x0), "core_far_1")]
    outs1 = product(1, spot, high, low, [n1, f1, *c1])
    h0 = add_half(*halves(x0), "x", second, "x_second_0")
    x1 = add_half(*outs1, "x", first, "x_first_1")
    c2 = [swap_core(n2, "core_near_2"), swap_core(after(f2, outs1, h0), "core_far_2")]
    outs2 = product(2, spot, high, low, [n2, f2, *c2])
    h1 = add_half(*halves(after(x1, outs2)), "x", second, "x_second_1")
    x2 = add_half(*outs2, "x", first, "x_first_2")
    h01 = jnp.stack([after(h0, outs2), h1])
    r01 = h01[:, :64] + swap(h01[:, 64:], "zh", across, "zh_01")
    h2 = add_half(*halves(x2), "x", second, "x_second_2")
    r2 = add_half(*halves(h2), "zh", across, "zh_2")
    return jnp.concatenate([r01, r2[None]])


def solution(mesh):
    mesh = Mesh(mesh.devices.reshape(SIZES), AXES)
    row, col = AXES[:2], AXES[2:]
    return jax.shard_map(
        local,
        mesh=mesh,
        in_specs=(P(None, AXES, None), P(None, row), P(None, col, row), P(None, col, row)),
        out_specs=P(None, col + row, None),
        check_vma=False,
    )
```

profile of v0, /device:TPU:32, one launch (start us, length us, event | category | flops | bytes accessed | tf_op | source)
XLA Modules:
  0.0 88.3 jit_solution(5159102340586448910)
XLA Ops:
  0.0 0.8 slice_bitcast_fusion.2
  0.8 3.3 %collective-permute-start = (f32[64,256]{1,0:T(8,128)S(1)}, f32[64,256]{1,0:T(8,128)S(1)}, u32[]{:S(2)}, u32[]{:S(2)}) collective-permute-start(f32[64,256]{1,0:T(8,128)S(1)} %slice_bitcast_fusion.2), channel_id=1, source_target_pairs={{0,16},{1,17},{8,24},{9,25},{16,0},{17,1},{24,8},{25,9},{2,18},{3,... | collective-permute-start | bytes 196616 | tf_op jit(solution)/shard_map/z_far_0/ppermute | solution.py:20
  4.1 2.3 %collective-permute-done = f32[64,256]{1,0:T(8,128)S(1)} collective-permute-done((f32[64,256]{1,0:T(8,128)S(1)}, f32[64,256]{1,0:T(8,128)S(1)}, u32[]{:S(2)}, u32[]{:S(2)}) %collective-permute-start) | collective-permute-done | bytes 65568 | tf_op jit(solution)/shard_map/z_far_0/ppermute | solution.py:20
  6.4 2.2 %collective-permute-start.1 = (f32[128,256]{1,0:T(8,128)S(1)}, f32[128,256]{1,0:T(8,128)S(1)}, u32[]{:S(2)}, u32[]{:S(2)}) collective-permute-start(f32[128,256]{1,0:T(8,128)S(1)} %pad_maximum_fusion.6), channel_id=1, source_target_pairs={{0,8},{1,9},{8,0},{9,1},{16,24},{17,25},{24,16},{25,17},{2,10},{3,... | collective-permute-start | bytes 393224 | tf_op jit(solution)/shard_map/z_near_0/ppermute | solution.py:20
  8.6 0.9 %slice.45 = f32[2,64,256]{2,1,0:T(8,128)S(1)} slice(f32[3,64,256]{2,1,0:T(8,128)} %param.4), slice={[1:3], [0:64], [0:256]} | slice | bytes 262144 | tf_op jit(solution)/shard_map/slice | solution.py:133
  9.5 1.4 %collective-permute-start.8 = (f32[2,64,256]{2,1,0:T(8,128)S(1)}, f32[2,64,256]{2,1,0:T(8,128)S(1)}, u32[]{:S(2)}, u32[]{:S(2)}) collective-permute-start(f32[2,64,256]{2,1,0:T(8,128)S(1)} %slice.45), channel_id=1, source_target_pairs={{0,16},{1,17},{8,24},{9,25},{16,0},{17,1},{24,8},{25,9},{2,18},{3,... | collective-permute-start | bytes 393224 | tf_op jit(solution)/shard_map/z_far_12/ppermute | solution.py:20
  10.9 1.0 %collective-permute-done.1 = f32[128,256]{1,0:T(8,128)S(1)} collective-permute-done((f32[128,256]{1,0:T(8,128)S(1)}, f32[128,256]{1,0:T(8,128)S(1)}, u32[]{:S(2)}, u32[]{:S(2)}) %collective-permute-start.1) | collective-permute-done | bytes 131104 | tf_op jit(solution)/shard_map/z_near_0/ppermute | solution.py:20
  11.9 1.3 %collective-permute-start.2 = (f32[256,256]{1,0:T(8,128)S(1)}, f32[256,256]{1,0:T(8,128)S(1)}, u32[]{:S(2)}, u32[]{:S(2)}) collective-permute-start(f32[256,256]{1,0:T(8,128)S(1)} %pad_maximum_fusion.2), channel_id=1, source_target_pairs={{0,2},{1,7},{2,0},{3,5},{4,6},{5,3},{6,4},{7,1},{8,10},{9,15},{10,... | collective-permute-start | bytes 786440 | tf_op jit(solution)/shard_map/y_first_0/ppermute | solution.py:20
  13.2 3.2 %collective-permute-done.8 = f32[2,64,256]{2,1,0:T(8,128)S(1)} collective-permute-done((f32[2,64,256]{2,1,0:T(8,128)S(1)}, f32[2,64,256]{2,1,0:T(8,128)S(1)}, u32[]{:S(2)}, u32[]{:S(2)}) %collective-permute-start.8) | collective-permute-done | bytes 131104 | tf_op jit(solution)/shard_map/z_far_12/ppermute | solution.py:20
  16.4 2.5 %collective-permute-start.9 = (f32[2,128,256]{2,1,0:T(8,128)S(1)}, f32[2,128,256]{2,1,0:T(8,128)S(1)}, u32[]{:S(2)}, u32[]{:S(2)}) collective-permute-start(f32[2,128,256]{2,1,0:T(8,128)S(1)} %pad_maximum_fusion.3), channel_id=1, source_target_pairs={{0,8},{1,9},{8,0},{9,1},{16,24},{17,25},{24,16},{25,17},{2,10},{3,... | collective-permute-start | bytes 786440 | tf_op jit(solution)/shard_map/z_near_12/ppermute | solution.py:20
  18.9 3.1 %collective-permute-start.3 = (f32[512,256]{1,0:T(8,128)S(1)}, f32[512,256]{1,0:T(8,128)S(1)}, u32[]{:S(2)}, u32[]{:S(2)}) collective-permute-start(f32[512,256]{1,0:T(8,128)S(1)} %pad_maximum_fusion.near), channel_id=1, source_target_pairs={{0,6},{1,3},{2,4},{3,1},{4,2},{5,7},{6,0},{7,5},{8,14},{9,11},{10,... | collective-permute-start | bytes 1572872 | tf_op jit(solution)/shard_map/y_second_0/ppermute | solution.py:20
  22.0 2.5 %collective-permute-done.9 = f32[2,128,256]{2,1,0:T(8,128)S(1)} collective-permute-done((f32[2,128,256]{2,1,0:T(8,128)S(1)}, f32[2,128,256]{2,1,0:T(8,128)S(1)}, u32[]{:S(2)}, u32[]{:S(2)}) %collective-permute-start.9) | collective-permute-done | bytes 262176 | tf_op jit(solution)/shard_map/z_near_12/ppermute | solution.py:20
  24.6 1.7 %collective-permute-start.10 = (f32[2,256,256]{2,1,0:T(8,128)S(1)}, f32[2,256,256]{2,1,0:T(8,128)S(1)}, u32[]{:S(2)}, u32[]{:S(2)}) collective-permute-start(f32[2,256,256]{2,1,0:T(8,128)S(1)} %pad_maximum_fusion.1), channel_id=1, source_target_pairs={{0,2},{1,7},{2,0},{3,5},{4,6},{5,3},{6,4},{7,1},{8,10},{9,15},{10,... | collective-permute-start | bytes 1572872 | tf_op jit(solution)/shard_map/y_first_12/ppermute | solution.py:20
  26.2 0.1 stack.32.spot
  26.3 0.7 convert_negate_fusion
  27.0 0.0 collective-permute-start.4
  27.0 0.1 broadcast_in_dim.7
  27.1 5.5 %split_tiles.1 = (bf16[3,512,2048]{2,1,0:T(8,128)(2,1)S(1)}, bf16[3,512,2048]{2,1,0:T(8,128)(2,1)S(1)}) custom-call(s32[5]{0:T(128)S(1)} %stack.32.spot, f32[3,4,1,2048]{3,2,1,0:T(1,128)S(1)} %bitcast.17, f32[3,512,2048]{2,1,0:T(8,128)} %tiles.1), custom_call_target="tpu_custom_call" | custom-call | tf_op jit(solution)/shard_map/split_tiles/pallas_call | solution.py:65
  32.6 0.0 collective-permute-done.3.far
  32.6 0.6 collective-permute-start.5
  33.2 0.6 collective-permute-done.10
  33.9 0.1 slice_bitcast_fusion
  34.0 3.1 %collective-permute-start.13 = (f32[512,256]{1,0:T(8,128)S(1)}, f32[512,256]{1,0:T(8,128)S(1)}, u32[]{:S(2)}, u32[]{:S(2)}) collective-permute-start(f32[512,256]{1,0:T(8,128)S(1)} %get-tuple-element.35.near), channel_id=1, source_target_pairs={{0,6},{1,3},{2,4},{3,1},{4,2},{5,7},{6,0},{7,5},{8,14},{9,11},{10,... | collective-permute-start | bytes 1572872 | tf_op jit(solution)/shard_map/y_second_1/ppermute | solution.py:20
  37.1 2.7 %product.3 = (f32[256,256]{1,0:T(8,128)S(1)}, f32[256,256]{1,0:T(8,128)S(1)}) custom-call(s32[5]{0:T(128)S(1)} %stack.32.spot, bf16[3,512,2048]{2,1,0:T(8,128)(2,1)S(1)} %get-tuple-element.21.high, bf16[3,512,2048]{2,1,0:T(8,128)(2,1)S(1)} %get-tuple-element.22.low, f32[512,256]{1,0:T(8,128)S(1)} %pad_maximum_fusion.near, ...), custom_call_target="tpu_custom_call" | custom-call | tf_op jit(solution)/shard_map/product/pallas_call | solution.py:100
  39.7 1.6 %collective-permute-start.6 = (f32[256,256]{1,0:T(8,128)S(1)}, f32[256,256]{1,0:T(8,128)S(1)}, u32[]{:S(2)}, u32[]{:S(2)}) collective-permute-start(f32[256,256]{1,0:T(8,128)S(1)} %get-tuple-element.25), channel_id=1, source_target_pairs={{0,32},{1,97},{32,0},{33,65},{64,96},{65,33},{96,64},{97,1},{2,34}... | collective-permute-start | bytes 786440 | tf_op jit(solution)/shard_map/x_first_0/ppermute | solution.py:20
  41.3 0.0 collective-permute-start.14
  41.3 4.9 %collective-permute-done.6 = f32[256,256]{1,0:T(8,128)S(1)} collective-permute-done((f32[256,256]{1,0:T(8,128)S(1)}, f32[256,256]{1,0:T(8,128)S(1)}, u32[]{:S(2)}, u32[]{:S(2)}) %collective-permute-start.6) | collective-permute-done | bytes 262176 | tf_op jit(solution)/shard_map/x_first_0/ppermute | solution.py:20
  46.2 0.0 collective-permute-done.13.far
  46.2 0.1 collective-permute-start.15
  46.3 1.4 %collective-permute-start.11 = (f32[512,256]{1,0:T(8,128)S(1)}, f32[512,256]{1,0:T(8,128)S(1)}, u32[]{:S(2)}, u32[]{:S(2)}) collective-permute-start(f32[512,256]{1,0:T(8,128)S(1)} %get-tuple-element.36.near), channel_id=1, source_target_pairs={{0,6},{1,3},{2,4},{3,1},{4,2},{5,7},{6,0},{7,5},{8,14},{9,11},{10,... | collective-permute-start | bytes 1572872 | tf_op jit(solution)/shard_map/y_second_2/ppermute | solution.py:20
  47.7 2.8 %collective-permute-start.7 = (f32[128,256]{1,0:T(8,128)S(1)}, f32[128,256]{1,0:T(8,128)S(1)}, u32[]{:S(2)}, u32[]{:S(2)}) collective-permute-start(f32[128,256]{1,0:T(8,128)S(1)} %slice.57), channel_id=1, source_target_pairs={{0,96},{1,33},{32,64},{33,1},{64,32},{65,97},{96,0},{97,65},{2,98}... | collective-permute-start | bytes 393224 | tf_op jit(solution)/shard_map/x_second_0/ppermute | solution.py:20
  50.6 0.0 collective-permute-start.12
  50.6 3.4 %collective-permute-done.7 = f32[128,256]{1,0:T(8,128)S(1)} collective-permute-done((f32[128,256]{1,0:T(8,128)S(1)}, f32[128,256]{1,0:T(8,128)S(1)}, u32[]{:S(2)}, u32[]{:S(2)}) %collective-permute-start.7) | collective-permute-done | bytes 131104 | tf_op jit(solution)/shard_map/x_second_0/ppermute | solution.py:20
  54.0 2.7 %product.4 = (f32[256,256]{1,0:T(8,128)S(1)}, f32[256,256]{1,0:T(8,128)S(1)}) custom-call(s32[5]{0:T(128)S(1)} %stack.32.spot, bf16[3,512,2048]{2,1,0:T(8,128)(2,1)S(1)} %get-tuple-element.21.high, bf16[3,512,2048]{2,1,0:T(8,128)(2,1)S(1)} %get-tuple-element.22.low, f32[512,256]{1,0:T(8,128)S(1)} %get-tuple-element.35.near, ...), custom_call_target="tpu_custom_call" | custom-call | tf_op jit(solution)/shard_map/product/pallas_call | solution.py:100
  56.7 0.1 collective-permute-done.11.far
  56.8 1.5 %collective-permute-start.17 = (f32[256,256]{1,0:T(8,128)S(1)}, f32[256,256]{1,0:T(8,128)S(1)}, u32[]{:S(2)}, u32[]{:S(2)}) collective-permute-start(f32[256,256]{1,0:T(8,128)S(1)} %get-tuple-element.29), channel_id=1, source_target_pairs={{0,32},{1,97},{32,0},{33,65},{64,96},{65,33},{96,64},{97,1},{2,34}... | collective-permute-start | bytes 786440 | tf_op jit(solution)/shard_map/x_first_1/ppermute | solution.py:20
  58.3 0.4 collective-permute-done.16.far_other
  58.7 2.7 %product.5 = (f32[256,256]{1,0:T(8,128)S(1)}, f32[256,256]{1,0:T(8,128)S(1)}) custom-call(s32[5]{0:T(128)S(1)} %stack.32.spot, bf16[3,512,2048]{2,1,0:T(8,128)(2,1)S(1)} %get-tuple-element.21.high, bf16[3,512,2048]{2,1,0:T(8,128)(2,1)S(1)} %get-tuple-element.22.low, f32[512,256]{1,0:T(8,128)S(1)} %get-tuple-element.36.near, ...), custom_call_target="tpu_custom_call" | custom-call | tf_op jit(solution)/shard_map/product/pallas_call | solution.py:100
  61.4 1.6 %collective-permute-start.20 = (f32[256,256]{1,0:T(8,128)S(1)}, f32[256,256]{1,0:T(8,128)S(1)}, u32[]{:S(2)}, u32[]{:S(2)}) collective-permute-start(f32[256,256]{1,0:T(8,128)S(1)} %get-tuple-element.32), channel_id=1, source_target_pairs={{0,32},{1,97},{32,0},{33,65},{64,96},{65,33},{96,64},{97,1},{2,34}... | collective-permute-start | bytes 786440 | tf_op jit(solution)/shard_map/x_first_2/ppermute | solution.py:20
  63.0 0.3 collective-permute-done.17
  63.3 2.9 %collective-permute-start.18 = (f32[128,256]{1,0:T(8,128)S(1)}, f32[128,256]{1,0:T(8,128)S(1)}, u32[]{:S(2)}, u32[]{:S(2)}) collective-permute-start(f32[128,256]{1,0:T(8,128)S(1)} %slice.49), channel_id=1, source_target_pairs={{0,96},{1,33},{32,64},{33,1},{64,32},{65,97},{96,0},{97,65},{2,98}... | collective-permute-start | bytes 393224 | tf_op jit(solution)/shard_map/x_second_1/ppermute | solution.py:20
  66.2 2.6 %collective-permute-done.20 = f32[256,256]{1,0:T(8,128)S(1)} collective-permute-done((f32[256,256]{1,0:T(8,128)S(1)}, f32[256,256]{1,0:T(8,128)S(1)}, u32[]{:S(2)}, u32[]{:S(2)}) %collective-permute-start.20) | collective-permute-done | bytes 262176 | tf_op jit(solution)/shard_map/x_first_2/ppermute | solution.py:20
  68.9 3.2 %collective-permute-start.21 = (f32[128,256]{1,0:T(8,128)S(1)}, f32[128,256]{1,0:T(8,128)S(1)}, u32[]{:S(2)}, u32[]{:S(2)}) collective-permute-start(f32[128,256]{1,0:T(8,128)S(1)} %slice.63), channel_id=1, source_target_pairs={{0,96},{1,33},{32,64},{33,1},{64,32},{65,97},{96,0},{97,65},{2,98}... | collective-permute-start | bytes 393224 | tf_op jit(solution)/shard_map/x_second_2/ppermute | solution.py:20
  72.1 6.6 %collective-permute-start.19 = (f32[2,64,256]{2,1,0:T(8,128)S(1)}, f32[2,64,256]{2,1,0:T(8,128)S(1)}, u32[]{:S(2)}, u32[]{:S(2)}) collective-permute-start(f32[2,64,256]{2,1,0:T(8,128)S(1)} %pad_maximum_fusion.5), channel_id=1, source_target_pairs={{0,128},{1,129},{128,0},{129,1},{2,130},{3,131},{130,2},{131,3},{4... | collective-permute-start | bytes 393224 | tf_op jit(solution)/shard_map/zh_01/ppermute | solution.py:20
  78.8 3.0 %collective-permute-start.22 = (f32[64,256]{1,0:T(8,128)S(1)}, f32[64,256]{1,0:T(8,128)S(1)}, u32[]{:S(2)}, u32[]{:S(2)}) collective-permute-start(f32[64,256]{1,0:T(8,128)S(1)} %slice.65), channel_id=1, source_target_pairs={{0,128},{1,129},{128,0},{129,1},{2,130},{3,131},{130,2},{131,3},{4... | collective-permute-start | bytes 196616 | tf_op jit(solution)/shard_map/zh_2/ppermute | solution.py:20
  81.8 1.4 %collective-permute-done.19 = f32[2,64,256]{2,1,0:T(8,128)S(1)} collective-permute-done((f32[2,64,256]{2,1,0:T(8,128)S(1)}, f32[2,64,256]{2,1,0:T(8,128)S(1)}, u32[]{:S(2)}, u32[]{:S(2)}) %collective-permute-start.19) | collective-permute-done | bytes 131104 | tf_op jit(solution)/shard_map/zh_01/ppermute | solution.py:20
  83.2 4.4 %collective-permute-done.22 = f32[64,256]{1,0:T(8,128)S(1)} collective-permute-done((f32[64,256]{1,0:T(8,128)S(1)}, f32[64,256]{1,0:T(8,128)S(1)}, u32[]{:S(2)}, u32[]{:S(2)}) %collective-permute-start.22) | collective-permute-done | bytes 65568 | tf_op jit(solution)/shard_map/zh_2/ppermute | solution.py:20
  87.6 0.7 pad_maximum_fusion.4
  (29 shorter events, 0.4 us)
Async XLA Ops:
  0.8 5.6 %collective-permute-start = (f32[64,256]{1,0:T(8,128)S(1)}, f32[64,256]{1,0:T(8,128)S(1)}, u32[]{:S(2)}, u32[]{:S(2)}) collective-permute-start(f32[64,256]{1,0:T(8,128)S(1)} %slice_bitcast_fusion.2), channel_id=1, source_target_pairs={{0,16},{1,17},{8,24},{9,25},{16,0},{17,1},{24,8},{25,9},{2,18},{3,... | collective-permute-start | bytes 196616 | tf_op jit(solution)/shard_map/z_far_0/ppermute | solution.py:20
  6.4 5.4 %collective-permute-start.1 = (f32[128,256]{1,0:T(8,128)S(1)}, f32[128,256]{1,0:T(8,128)S(1)}, u32[]{:S(2)}, u32[]{:S(2)}) collective-permute-start(f32[128,256]{1,0:T(8,128)S(1)} %pad_maximum_fusion.6), channel_id=1, source_target_pairs={{0,8},{1,9},{8,0},{9,1},{16,24},{17,25},{24,16},{25,17},{2,10},{3,... | collective-permute-start | bytes 393224 | tf_op jit(solution)/shard_map/z_near_0/ppermute | solution.py:20
  9.5 6.8 %collective-permute-start.8 = (f32[2,64,256]{2,1,0:T(8,128)S(1)}, f32[2,64,256]{2,1,0:T(8,128)S(1)}, u32[]{:S(2)}, u32[]{:S(2)}) collective-permute-start(f32[2,64,256]{2,1,0:T(8,128)S(1)} %slice.45), channel_id=1, source_target_pairs={{0,16},{1,17},{8,24},{9,25},{16,0},{17,1},{24,8},{25,9},{2,18},{3,... | collective-permute-start | bytes 393224 | tf_op jit(solution)/shard_map/z_far_12/ppermute | solution.py:20
  11.9 7.0 %collective-permute-start.2 = (f32[256,256]{1,0:T(8,128)S(1)}, f32[256,256]{1,0:T(8,128)S(1)}, u32[]{:S(2)}, u32[]{:S(2)}) collective-permute-start(f32[256,256]{1,0:T(8,128)S(1)} %pad_maximum_fusion.2), channel_id=1, source_target_pairs={{0,2},{1,7},{2,0},{3,5},{4,6},{5,3},{6,4},{7,1},{8,10},{9,15},{10,... | collective-permute-start | bytes 786440 | tf_op jit(solution)/shard_map/y_first_0/ppermute | solution.py:20
  16.4 8.2 %collective-permute-start.9 = (f32[2,128,256]{2,1,0:T(8,128)S(1)}, f32[2,128,256]{2,1,0:T(8,128)S(1)}, u32[]{:S(2)}, u32[]{:S(2)}) collective-permute-start(f32[2,128,256]{2,1,0:T(8,128)S(1)} %pad_maximum_fusion.3), channel_id=1, source_target_pairs={{0,8},{1,9},{8,0},{9,1},{16,24},{17,25},{24,16},{25,17},{2,10},{3,... | collective-permute-start | bytes 786440 | tf_op jit(solution)/shard_map/z_near_12/ppermute | solution.py:20
  18.9 13.7 %collective-permute-start.3 = (f32[512,256]{1,0:T(8,128)S(1)}, f32[512,256]{1,0:T(8,128)S(1)}, u32[]{:S(2)}, u32[]{:S(2)}) collective-permute-start(f32[512,256]{1,0:T(8,128)S(1)} %pad_maximum_fusion.near), channel_id=1, source_target_pairs={{0,6},{1,3},{2,4},{3,1},{4,2},{5,7},{6,0},{7,5},{8,14},{9,11},{10,... | collective-permute-start | bytes 1572872 | tf_op jit(solution)/shard_map/y_second_0/ppermute | solution.py:20
  24.6 9.3 %collective-permute-start.10 = (f32[2,256,256]{2,1,0:T(8,128)S(1)}, f32[2,256,256]{2,1,0:T(8,128)S(1)}, u32[]{:S(2)}, u32[]{:S(2)}) collective-permute-start(f32[2,256,256]{2,1,0:T(8,128)S(1)} %pad_maximum_fusion.1), channel_id=1, source_target_pairs={{0,2},{1,7},{2,0},{3,5},{4,6},{5,3},{6,4},{7,1},{8,10},{9,15},{10,... | collective-permute-start | bytes 1572872 | tf_op jit(solution)/shard_map/y_first_12/ppermute | solution.py:20
  27.0 10.0 %collective-permute-start.4 = (f32[512,256]{1,0:T(8,128)S(1)}, f32[512,256]{1,0:T(8,128)S(1)}, u32[]{:S(2)}, u32[]{:S(2)}) collective-permute-start(f32[512,256]{1,0:T(8,128)S(1)} %pad_maximum_fusion.near), channel_id=1, source_target_pairs={{0,1},{1,0},{2,3},{3,2},{4,5},{5,4},{6,7},{7,6},{8,9},{9,8},{10,11... | collective-permute-start | bytes 1572872 | tf_op jit(solution)/shard_map/core_near_0/ppermute | solution.py:25
  32.6 4.4 %collective-permute-start.5 = (f32[512,256]{1,0:T(8,128)S(1)}, f32[512,256]{1,0:T(8,128)S(1)}, u32[]{:S(2)}, u32[]{:S(2)}) collective-permute-start(f32[512,256]{1,0:T(8,128)S(1)} %collective-permute-done.3.far), channel_id=1, source_target_pairs={{0,1},{1,0},{2,3},{3,2},{4,5},{5,4},{6,7},{7,6},{8,9},{9,8},{10,11... | collective-permute-start | bytes 1572872 | tf_op jit(solution)/shard_map/core_far_0/ppermute | solution.py:25
  34.0 12.3 %collective-permute-start.13 = (f32[512,256]{1,0:T(8,128)S(1)}, f32[512,256]{1,0:T(8,128)S(1)}, u32[]{:S(2)}, u32[]{:S(2)}) collective-permute-start(f32[512,256]{1,0:T(8,128)S(1)} %get-tuple-element.35.near), channel_id=1, source_target_pairs={{0,6},{1,3},{2,4},{3,1},{4,2},{5,7},{6,0},{7,5},{8,14},{9,11},{10,... | collective-permute-start | bytes 1572872 | tf_op jit(solution)/shard_map/y_second_1/ppermute | solution.py:20
  39.7 6.5 %collective-permute-start.6 = (f32[256,256]{1,0:T(8,128)S(1)}, f32[256,256]{1,0:T(8,128)S(1)}, u32[]{:S(2)}, u32[]{:S(2)}) collective-permute-start(f32[256,256]{1,0:T(8,128)S(1)} %get-tuple-element.25), channel_id=1, source_target_pairs={{0,32},{1,97},{32,0},{33,65},{64,96},{65,33},{96,64},{97,1},{2,34}... | collective-permute-start | bytes 786440 | tf_op jit(solution)/shard_map/x_first_0/ppermute | solution.py:20
  41.3 12.7 %collective-permute-start.14 = (f32[512,256]{1,0:T(8,128)S(1)}, f32[512,256]{1,0:T(8,128)S(1)}, u32[]{:S(2)}, u32[]{:S(2)}) collective-permute-start(f32[512,256]{1,0:T(8,128)S(1)} %get-tuple-element.35.near), channel_id=1, source_target_pairs={{0,1},{1,0},{2,3},{3,2},{4,5},{5,4},{6,7},{7,6},{8,9},{9,8},{10,11... | collective-permute-start | bytes 1572872 | tf_op jit(solution)/shard_map/core_near_1/ppermute | solution.py:25
  46.2 7.8 %collective-permute-start.15 = (f32[512,256]{1,0:T(8,128)S(1)}, f32[512,256]{1,0:T(8,128)S(1)}, u32[]{:S(2)}, u32[]{:S(2)}) collective-permute-start(f32[512,256]{1,0:T(8,128)S(1)} %collective-permute-done.13.far), channel_id=1, source_target_pairs={{0,1},{1,0},{2,3},{3,2},{4,5},{5,4},{6,7},{7,6},{8,9},{9,8},{10,11... | collective-permute-start | bytes 1572872 | tf_op jit(solution)/shard_map/core_far_1/ppermute | solution.py:25
  46.3 10.5 %collective-permute-start.11 = (f32[512,256]{1,0:T(8,128)S(1)}, f32[512,256]{1,0:T(8,128)S(1)}, u32[]{:S(2)}, u32[]{:S(2)}) collective-permute-start(f32[512,256]{1,0:T(8,128)S(1)} %get-tuple-element.36.near), channel_id=1, source_target_pairs={{0,6},{1,3},{2,4},{3,1},{4,2},{5,7},{6,0},{7,5},{8,14},{9,11},{10,... | collective-permute-start | bytes 1572872 | tf_op jit(solution)/shard_map/y_second_2/ppermute | solution.py:20
  47.7 6.3 %collective-permute-start.7 = (f32[128,256]{1,0:T(8,128)S(1)}, f32[128,256]{1,0:T(8,128)S(1)}, u32[]{:S(2)}, u32[]{:S(2)}) collective-permute-start(f32[128,256]{1,0:T(8,128)S(1)} %slice.57), channel_id=1, source_target_pairs={{0,96},{1,33},{32,64},{33,1},{64,32},{65,97},{96,0},{97,65},{2,98}... | collective-permute-start | bytes 393224 | tf_op jit(solution)/shard_map/x_second_0/ppermute | solution.py:20
  50.6 7.7 %collective-permute-start.12 = (f32[512,256]{1,0:T(8,128)S(1)}, f32[512,256]{1,0:T(8,128)S(1)}, u32[]{:S(2)}, u32[]{:S(2)}) collective-permute-start(f32[512,256]{1,0:T(8,128)S(1)} %get-tuple-element.36.near), channel_id=1, source_target_pairs={{0,1},{1,0},{2,3},{3,2},{4,5},{5,4},{6,7},{7,6},{8,9},{9,8},{10,11... | collective-permute-start | bytes 1572872 | tf_op jit(solution)/shard_map/core_near_2/ppermute | solution.py:25
  56.8 1.9 %collective-permute-start.16 = (f32[512,256]{1,0:T(8,128)S(1)}, f32[512,256]{1,0:T(8,128)S(1)}, u32[]{:S(2)}, u32[]{:S(2)}) collective-permute-start(f32[512,256]{1,0:T(8,128)S(1)} %collective-permute-done.11.far), channel_id=1, source_target_pairs={{0,1},{1,0},{2,3},{3,2},{4,5},{5,4},{6,7},{7,6},{8,9},{9,8},{10,11... | collective-permute-start | bytes 1572872 | tf_op jit(solution)/shard_map/core_far_2/ppermute | solution.py:25
  56.8 6.4 %collective-permute-start.17 = (f32[256,256]{1,0:T(8,128)S(1)}, f32[256,256]{1,0:T(8,128)S(1)}, u32[]{:S(2)}, u32[]{:S(2)}) collective-permute-start(f32[256,256]{1,0:T(8,128)S(1)} %get-tuple-element.29), channel_id=1, source_target_pairs={{0,32},{1,97},{32,0},{33,65},{64,96},{65,33},{96,64},{97,1},{2,34}... | collective-permute-start | bytes 786440 | tf_op jit(solution)/shard_map/x_first_1/ppermute | solution.py:20
  61.4 7.4 %collective-permute-start.20 = (f32[256,256]{1,0:T(8,128)S(1)}, f32[256,256]{1,0:T(8,128)S(1)}, u32[]{:S(2)}, u32[]{:S(2)}) collective-permute-start(f32[256,256]{1,0:T(8,128)S(1)} %get-tuple-element.32), channel_id=1, source_target_pairs={{0,32},{1,97},{32,0},{33,65},{64,96},{65,33},{96,64},{97,1},{2,34}... | collective-permute-start | bytes 786440 | tf_op jit(solution)/shard_map/x_first_2/ppermute | solution.py:20
  63.3 8.7 %collective-permute-start.18 = (f32[128,256]{1,0:T(8,128)S(1)}, f32[128,256]{1,0:T(8,128)S(1)}, u32[]{:S(2)}, u32[]{:S(2)}) collective-permute-start(f32[128,256]{1,0:T(8,128)S(1)} %slice.49), channel_id=1, source_target_pairs={{0,96},{1,33},{32,64},{33,1},{64,32},{65,97},{96,0},{97,65},{2,98}... | collective-permute-start | bytes 393224 | tf_op jit(solution)/shard_map/x_second_1/ppermute | solution.py:20
  68.9 9.9 %collective-permute-start.21 = (f32[128,256]{1,0:T(8,128)S(1)}, f32[128,256]{1,0:T(8,128)S(1)}, u32[]{:S(2)}, u32[]{:S(2)}) collective-permute-start(f32[128,256]{1,0:T(8,128)S(1)} %slice.63), channel_id=1, source_target_pairs={{0,96},{1,33},{32,64},{33,1},{64,32},{65,97},{96,0},{97,65},{2,98}... | collective-permute-start | bytes 393224 | tf_op jit(solution)/shard_map/x_second_2/ppermute | solution.py:20
  72.1 11.1 %collective-permute-start.19 = (f32[2,64,256]{2,1,0:T(8,128)S(1)}, f32[2,64,256]{2,1,0:T(8,128)S(1)}, u32[]{:S(2)}, u32[]{:S(2)}) collective-permute-start(f32[2,64,256]{2,1,0:T(8,128)S(1)} %pad_maximum_fusion.5), channel_id=1, source_target_pairs={{0,128},{1,129},{128,0},{129,1},{2,130},{3,131},{130,2},{131,3},{4... | collective-permute-start | bytes 393224 | tf_op jit(solution)/shard_map/zh_01/ppermute | solution.py:20
  78.8 8.8 %collective-permute-start.22 = (f32[64,256]{1,0:T(8,128)S(1)}, f32[64,256]{1,0:T(8,128)S(1)}, u32[]{:S(2)}, u32[]{:S(2)}) collective-permute-start(f32[64,256]{1,0:T(8,128)S(1)} %slice.65), channel_id=1, source_target_pairs={{0,128},{1,129},{128,0},{129,1},{2,130},{3,131},{130,2},{131,3},{4... | collective-permute-start | bytes 196616 | tf_op jit(solution)/shard_map/zh_2/ppermute | solution.py:20
where the time goes:
time: 88.8 us; the launch traced here: 88.3 us
  starting transfers between devices  43.7 us (49%)
  waiting for transfers between devices  27.1 us (31%)
  Pallas kernels  13.4 us (15%)
  local copies, waits for them, and re-layouts  2.1 us (2%)
  other arithmetic  1.7 us (2%)
    ppermute x17, starting transfers between devices, swap(): return lax.ppermute(value, (axis, 'core'), pairs)  43 us
    ppermute x17, waiting for transfers between devices, swap(): return lax.ppermute(value, (axis, 'core'), pairs)  26.7 us
    pallas_call x3, Pallas kernels, product(): pl.pallas_call(functools.partial(product_kernel, n), out_shape=[jax.Shape...  7.98 us
    pallas_call x1, Pallas kernels, split_tiles(): pl.pallas_call(tiles_kernel, out_shape=[out, out], in_specs=[pl.BlockSpec...  5.45 us
  transfers between devices with their start and end apart: 23, of which 13 were waited for; matrix products, arithmetic and copies ran while one was open for 3% of the time, Pallas kernels for 15%

commit v1 on v0

--- a/solution.py
+++ b/solution.py
@@ -129,9 +129,9 @@
 
     near_z, far_z, first, second, across = (1, 1), (2, 2), (1, 3), (3, 1), (1, 1)
 
-    a0 = grow(lower_panel[0], "zl", far_z, "z_far_0")
+    own = lower_panel[0]
+    g0 = jnp.concatenate([own] + [swap(own, "zl", (dz, dz), "z_{}_0".format(dz)) for dz in (2, 1, 3)])
     a12 = grow(lower_panel[1:], "zl", far_z, "z_far_12")
-    g0 = grow(a0, "zl", near_z, "z_near_0")
     g12 = grow(a12, "zl", near_z, "z_near_12")
     n0 = grow(g0, "y", first, "y_first_0")
     high, low = split_tiles(spot, inverse_tiles, after(factors, n0))
@@ -146,7 +146,7 @@
     outs1 = product(1, spot, high, low, [n1, f1, *c1])
     h0 = add_half(*halves(x0), "x", second, "x_second_0")
     x1 = add_half(*outs1, "x", first, "x_first_1")
-    c2 = [swap_core(n2, "core_near_2"), swap_core(after(f2, outs1, h0), "core_far_2")]
+    c2 = [swap_core(n2, "core_near_2"), swap_core(after(f2, outs1), "core_far_2")]
     outs2 = product(2, spot, high, low, [n2, f2, *c2])
     h1 = add_half(*halves(after(x1, outs2)), "x", second, "x_second_1")
     x2 = add_half(*outs2, "x", first, "x_first_2")

time: 88.8 us -> 87.8 us (0.989)
  waiting for transfers between devices: 27.1 us -> 23.2 us
  starting transfers between devices: 43.7 us -> 45.6 us
    ppermute x17 -> x18, waiting for transfers between devices: 26.7 us -> 23.2 us  [swap(): return lax.ppermute(value, (axis, 'core'), pairs)]
    ppermute x17 -> x18, starting transfers between devices: 43 us -> 44.7 us  [swap(): return lax.ppermute(value, (axis, 'core'), pairs)]
  transfers between devices with their start and end apart: 23 -> 24, of which waited for: 13 -> 10; matrix products, arithmetic and copies ran while one was open for 3% -> 4% of each run, Pallas kernels for 15% -> 15%
where the time goes in v1:
time: 87.8 us; the launch traced here: 87.1 us
  starting transfers between devices  45.6 us (52%)
  waiting for transfers between devices  23.2 us (26%)
  Pallas kernels  13.4 us (15%)
  local copies, waits for them, and re-layouts  2.97 us (3%)
  other arithmetic  1.66 us (2%)
    ppermute x18, starting transfers between devices, swap(): return lax.ppermute(value, (axis, 'core'), pairs)  44.7 us
    ppermute x18, waiting for transfers between devices, swap(): return lax.ppermute(value, (axis, 'core'), pairs)  23.2 us
    pallas_call x3, Pallas kernels, product(): pl.pallas_call(functools.partial(product_kernel, n), out_shape=[jax.Shape...  7.99 us
    pallas_call x1, Pallas kernels, split_tiles(): pl.pallas_call(tiles_kernel, out_shape=[out, out], in_specs=[pl.BlockSpec...  5.45 us
  transfers between devices with their start and end apart: 24, of which 10 were waited for; matrix products, arithmetic and copies ran while one was open for 4% of the time, Pallas kernels for 15%

profile of v1, /device:TPU:32, one launch (start us, length us, event | category | flops | bytes accessed | tf_op | source)
XLA Modules:
  0.0 87.1 jit_solution(5758180590213910070)
XLA Ops:
  0.0 0.8 slice_bitcast_fusion.2
  0.8 3.3 %collective-permute-start = (f32[64,256]{1,0:T(8,128)S(1)}, f32[64,256]{1,0:T(8,128)S(1)}, u32[]{:S(2)}, u32[]{:S(2)}) collective-permute-start(f32[64,256]{1,0:T(8,128)S(1)} %slice_bitcast_fusion.2), channel_id=1, source_target_pairs={{0,16},{1,17},{8,24},{9,25},{16,0},{17,1},{24,8},{25,9},{2,18},{3,... | collective-permute-start | bytes 196616 | tf_op jit(solution)/shard_map/z_2_0/ppermute | solution.py:20
  4.1 0.1 collective-permute-start.1
  4.2 0.5 collective-permute-start.2
  4.7 0.9 %slice.45 = f32[2,64,256]{2,1,0:T(8,128)S(1)} slice(f32[3,64,256]{2,1,0:T(8,128)} %param.4), slice={[1:3], [0:64], [0:256]} | slice | bytes 262144 | tf_op jit(solution)/shard_map/slice | solution.py:134
  5.6 3.9 %collective-permute-start.9 = (f32[2,64,256]{2,1,0:T(8,128)S(1)}, f32[2,64,256]{2,1,0:T(8,128)S(1)}, u32[]{:S(2)}, u32[]{:S(2)}) collective-permute-start(f32[2,64,256]{2,1,0:T(8,128)S(1)} %slice.45), channel_id=1, source_target_pairs={{0,16},{1,17},{8,24},{9,25},{16,0},{17,1},{24,8},{25,9},{2,18},{3,... | collective-permute-start | bytes 393224 | tf_op jit(solution)/shard_map/z_far_12/ppermute | solution.py:20
  9.5 0.8 constant_dynamic-update-slice_fusion.4
  10.4 0.0 collective-permute-done.1
  10.4 2.1 %collective-permute-done.2 = f32[64,256]{1,0:T(8,128)S(1)} collective-permute-done((f32[64,256]{1,0:T(8,128)S(1)}, f32[64,256]{1,0:T(8,128)S(1)}, u32[]{:S(2)}, u32[]{:S(2)}) %collective-permute-start.2) | collective-permute-done | bytes 65568 | tf_op jit(solution)/shard_map/z_3_0/ppermute | solution.py:20
  12.5 1.7 %collective-permute-start.3 = (f32[256,256]{1,0:T(8,128)S(1)}, f32[256,256]{1,0:T(8,128)S(1)}, u32[]{:S(2)}, u32[]{:S(2)}) collective-permute-start(f32[256,256]{1,0:T(8,128)S(1)} %pad_maximum_fusion.1), channel_id=1, source_target_pairs={{0,2},{1,7},{2,0},{3,5},{4,6},{5,3},{6,4},{7,1},{8,10},{9,15},{10,... | collective-permute-start | bytes 786440 | tf_op jit(solution)/shard_map/y_first_0/ppermute | solution.py:20
  14.2 0.7 collective-permute-done.9
  14.9 2.2 %collective-permute-start.10 = (f32[2,128,256]{2,1,0:T(8,128)S(1)}, f32[2,128,256]{2,1,0:T(8,128)S(1)}, u32[]{:S(2)}, u32[]{:S(2)}) collective-permute-start(f32[2,128,256]{2,1,0:T(8,128)S(1)} %pad_maximum_fusion.2), channel_id=1, source_target_pairs={{0,8},{1,9},{8,0},{9,1},{16,24},{17,25},{24,16},{25,17},{2,10},{3,... | collective-permute-start | bytes 786440 | tf_op jit(solution)/shard_map/z_near_12/ppermute | solution.py:20
  17.1 1.9 %collective-permute-done.3 = f32[256,256]{1,0:T(8,128)S(1)} collective-permute-done((f32[256,256]{1,0:T(8,128)S(1)}, f32[256,256]{1,0:T(8,128)S(1)}, u32[]{:S(2)}, u32[]{:S(2)}) %collective-permute-start.3) | collective-permute-done | bytes 262176 | tf_op jit(solution)/shard_map/y_first_0/ppermute | solution.py:20
  19.0 3.1 %collective-permute-start.4 = (f32[512,256]{1,0:T(8,128)S(1)}, f32[512,256]{1,0:T(8,128)S(1)}, u32[]{:S(2)}, u32[]{:S(2)}) collective-permute-start(f32[512,256]{1,0:T(8,128)S(1)} %constant_dynamic-update-slice_fusion.near), channel_id=1, source_target_pairs={{0,6},{1,3},{2,4},{3,1},{4,2},{5,7},{6,0},{7,5},{8,14},{9,11},{10,... | collective-permute-start | bytes 1572872 | tf_op jit(solution)/shard_map/y_second_0/ppermute | solution.py:20
  22.1 1.4 %collective-permute-done.10 = f32[2,128,256]{2,1,0:T(8,128)S(1)} collective-permute-done((f32[2,128,256]{2,1,0:T(8,128)S(1)}, f32[2,128,256]{2,1,0:T(8,128)S(1)}, u32[]{:S(2)}, u32[]{:S(2)}) %collective-permute-start.10) | collective-permute-done | bytes 262176 | tf_op jit(solution)/shard_map/z_near_12/ppermute | solution.py:20
  23.5 1.7 %collective-permute-start.11 = (f32[2,256,256]{2,1,0:T(8,128)S(1)}, f32[2,256,256]{2,1,0:T(8,128)S(1)}, u32[]{:S(2)}, u32[]{:S(2)}) collective-permute-start(f32[2,256,256]{2,1,0:T(8,128)S(1)} %pad_maximum_fusion), channel_id=1, source_target_pairs={{0,2},{1,7},{2,0},{3,5},{4,6},{5,3},{6,4},{7,1},{8,10},{9,15},{10,... | collective-permute-start | bytes 1572872 | tf_op jit(solution)/shard_map/y_first_12/ppermute | solution.py:20
  25.2 0.1 stack.32.spot
  25.3 0.7 convert_negate_fusion
  26.0 0.6 collective-permute-start.5
  26.6 0.1 broadcast_in_dim.7
  26.7 5.5 %split_tiles.1 = (bf16[3,512,2048]{2,1,0:T(8,128)(2,1)S(1)}, bf16[3,512,2048]{2,1,0:T(8,128)(2,1)S(1)}) custom-call(s32[5]{0:T(128)S(1)} %stack.32.spot, f32[3,4,1,2048]{3,2,1,0:T(1,128)S(1)} %bitcast.19, f32[3,512,2048]{2,1,0:T(8,128)} %tiles.1), custom_call_target="tpu_custom_call" | custom-call | tf_op jit(solution)/shard_map/split_tiles/pallas_call | solution.py:65
  32.2 0.0 collective-permute-done.4.far
  32.2 0.1 collective-permute-start.6
  32.3 0.5 collective-permute-done.11
  32.9 0.1 slice_bitcast_fusion
  32.9 3.1 %collective-permute-start.14 = (f32[512,256]{1,0:T(8,128)S(1)}, f32[512,256]{1,0:T(8,128)S(1)}, u32[]{:S(2)}, u32[]{:S(2)}) collective-permute-start(f32[512,256]{1,0:T(8,128)S(1)} %get-tuple-element.35.near), channel_id=1, source_target_pairs={{0,6},{1,3},{2,4},{3,1},{4,2},{5,7},{6,0},{7,5},{8,14},{9,11},{10,... | collective-permute-start | bytes 1572872 | tf_op jit(solution)/shard_map/y_second_1/ppermute | solution.py:20
  36.0 0.0 collective-permute-done.5.near_other
  36.0 2.7 %product.3 = (f32[256,256]{1,0:T(8,128)S(1)}, f32[256,256]{1,0:T(8,128)S(1)}) custom-call(s32[5]{0:T(128)S(1)} %stack.32.spot, bf16[3,512,2048]{2,1,0:T(8,128)(2,1)S(1)} %get-tuple-element.21.high, bf16[3,512,2048]{2,1,0:T(8,128)(2,1)S(1)} %get-tuple-element.22.low, f32[512,256]{1,0:T(8,128)S(1)} %constant_dynamic-update-slice_fusion.near, ...), custom_call_target="tpu_custom_call" | custom-call | tf_op jit(solution)/shard_map/product/pallas_call | solution.py:100
  38.7 1.6 %collective-permute-start.7 = (f32[256,256]{1,0:T(8,128)S(1)}, f32[256,256]{1,0:T(8,128)S(1)}, u32[]{:S(2)}, u32[]{:S(2)}) collective-permute-start(f32[256,256]{1,0:T(8,128)S(1)} %get-tuple-element.25), channel_id=1, source_target_pairs={{0,32},{1,97},{32,0},{33,65},{64,96},{65,33},{96,64},{97,1},{2,34}... | collective-permute-start | bytes 786440 | tf_op jit(solution)/shard_map/x_first_0/ppermute | solution.py:20
  40.3 0.1 collective-permute-start.15
  40.4 4.7 %collective-permute-done.7 = f32[256,256]{1,0:T(8,128)S(1)} collective-permute-done((f32[256,256]{1,0:T(8,128)S(1)}, f32[256,256]{1,0:T(8,128)S(1)}, u32[]{:S(2)}, u32[]{:S(2)}) %collective-permute-start.7) | collective-permute-done | bytes 262176 | tf_op jit(solution)/shard_map/x_first_0/ppermute | solution.py:20
  45.2 0.1 collective-permute-start.16
  45.3 2.2 %collective-permute-start.12 = (f32[512,256]{1,0:T(8,128)S(1)}, f32[512,256]{1,0:T(8,128)S(1)}, u32[]{:S(2)}, u32[]{:S(2)}) collective-permute-start(f32[512,256]{1,0:T(8,128)S(1)} %get-tuple-element.36.near), channel_id=1, source_target_pairs={{0,6},{1,3},{2,4},{3,1},{4,2},{5,7},{6,0},{7,5},{8,14},{9,11},{10,... | collective-permute-start | bytes 1572872 | tf_op jit(solution)/shard_map/y_second_2/ppermute | solution.py:20
  47.5 0.0 collective-permute-start.13
  47.5 2.7 %product.4 = (f32[256,256]{1,0:T(8,128)S(1)}, f32[256,256]{1,0:T(8,128)S(1)}) custom-call(s32[5]{0:T(128)S(1)} %stack.32.spot, bf16[3,512,2048]{2,1,0:T(8,128)(2,1)S(1)} %get-tuple-element.21.high, bf16[3,512,2048]{2,1,0:T(8,128)(2,1)S(1)} %get-tuple-element.22.low, f32[512,256]{1,0:T(8,128)S(1)} %get-tuple-element.35.near, ...), custom_call_target="tpu_custom_call" | custom-call | tf_op jit(solution)/shard_map/product/pallas_call | solution.py:100
  50.2 5.6 %collective-permute-done.12.far = f32[512,256]{1,0:T(8,128)S(1)} collective-permute-done((f32[512,256]{1,0:T(8,128)S(1)}, f32[512,256]{1,0:T(8,128)S(1)}, u32[]{:S(2)}, u32[]{:S(2)}) %collective-permute-start.12) | collective-permute-done | bytes 524320 | tf_op jit(solution)/shard_map/y_second_2/ppermute | solution.py:20
  55.8 1.5 %collective-permute-start.18 = (f32[256,256]{1,0:T(8,128)S(1)}, f32[256,256]{1,0:T(8,128)S(1)}, u32[]{:S(2)}, u32[]{:S(2)}) collective-permute-start(f32[256,256]{1,0:T(8,128)S(1)} %get-tuple-element.29), channel_id=1, source_target_pairs={{0,32},{1,97},{32,0},{33,65},{64,96},{65,33},{96,64},{97,1},{2,34}... | collective-permute-start | bytes 786440 | tf_op jit(solution)/shard_map/x_first_1/ppermute | solution.py:20
  57.3 2.2 %collective-permute-start.8 = (f32[128,256]{1,0:T(8,128)S(1)}, f32[128,256]{1,0:T(8,128)S(1)}, u32[]{:S(2)}, u32[]{:S(2)}) collective-permute-start(f32[128,256]{1,0:T(8,128)S(1)} %slice.57), channel_id=1, source_target_pairs={{0,96},{1,33},{32,64},{33,1},{64,32},{65,97},{96,0},{97,65},{2,98}... | collective-permute-start | bytes 393224 | tf_op jit(solution)/shard_map/x_second_0/ppermute | solution.py:20
  59.5 2.7 %product.5 = (f32[256,256]{1,0:T(8,128)S(1)}, f32[256,256]{1,0:T(8,128)S(1)}) custom-call(s32[5]{0:T(128)S(1)} %stack.32.spot, bf16[3,512,2048]{2,1,0:T(8,128)(2,1)S(1)} %get-tuple-element.21.high, bf16[3,512,2048]{2,1,0:T(8,128)(2,1)S(1)} %get-tuple-element.22.low, f32[512,256]{1,0:T(8,128)S(1)} %get-tuple-element.36.near, ...), custom_call_target="tpu_custom_call" | custom-call | tf_op jit(solution)/shard_map/product/pallas_call | solution.py:100
  62.2 0.7 collective-permute-start.21
  62.9 3.4 %collective-permute-start.19 = (f32[128,256]{1,0:T(8,128)S(1)}, f32[128,256]{1,0:T(8,128)S(1)}, u32[]{:S(2)}, u32[]{:S(2)}) collective-permute-start(f32[128,256]{1,0:T(8,128)S(1)} %slice.49), channel_id=1, source_target_pairs={{0,96},{1,33},{32,64},{33,1},{64,32},{65,97},{96,0},{97,65},{2,98}... | collective-permute-start | bytes 393224 | tf_op jit(solution)/shard_map/x_second_1/ppermute | solution.py:20
  66.3 3.7 %collective-permute-done.21 = f32[256,256]{1,0:T(8,128)S(1)} collective-permute-done((f32[256,256]{1,0:T(8,128)S(1)}, f32[256,256]{1,0:T(8,128)S(1)}, u32[]{:S(2)}, u32[]{:S(2)}) %collective-permute-start.21) | collective-permute-done | bytes 262176 | tf_op jit(solution)/shard_map/x_first_2/ppermute | solution.py:20
  70.1 0.1 collective-permute-start.22
  70.2 7.5 %collective-permute-start.20 = (f32[2,64,256]{2,1,0:T(8,128)S(1)}, f32[2,64,256]{2,1,0:T(8,128)S(1)}, u32[]{:S(2)}, u32[]{:S(2)}) collective-permute-start(f32[2,64,256]{2,1,0:T(8,128)S(1)} %pad_maximum_fusion.4), channel_id=1, source_target_pairs={{0,128},{1,129},{128,0},{129,1},{2,130},{3,131},{130,2},{131,3},{4... | collective-permute-start | bytes 393224 | tf_op jit(solution)/shard_map/zh_01/ppermute | solution.py:20
  77.8 6.1 %collective-permute-start.23 = (f32[64,256]{1,0:T(8,128)S(1)}, f32[64,256]{1,0:T(8,128)S(1)}, u32[]{:S(2)}, u32[]{:S(2)}) collective-permute-start(f32[64,256]{1,0:T(8,128)S(1)} %slice.65), channel_id=1, source_target_pairs={{0,128},{1,129},{128,0},{129,1},{2,130},{3,131},{130,2},{131,3},{4... | collective-permute-start | bytes 196616 | tf_op jit(solution)/shard_map/zh_2/ppermute | solution.py:20
  83.9 0.3 collective-permute-done.20
  84.2 2.2 %collective-permute-done.23 = f32[64,256]{1,0:T(8,128)S(1)} collective-permute-done((f32[64,256]{1,0:T(8,128)S(1)}, f32[64,256]{1,0:T(8,128)S(1)}, u32[]{:S(2)}, u32[]{:S(2)}) %collective-permute-start.23) | collective-permute-done | bytes 65568 | tf_op jit(solution)/shard_map/zh_2/ppermute | solution.py:20
  86.4 0.7 pad_maximum_fusion.3
  (34 shorter events, 0.4 us)
Async XLA Ops:
  0.8 9.5 %collective-permute-start = (f32[64,256]{1,0:T(8,128)S(1)}, f32[64,256]{1,0:T(8,128)S(1)}, u32[]{:S(2)}, u32[]{:S(2)}) collective-permute-start(f32[64,256]{1,0:T(8,128)S(1)} %slice_bitcast_fusion.2), channel_id=1, source_target_pairs={{0,16},{1,17},{8,24},{9,25},{16,0},{17,1},{24,8},{25,9},{2,18},{3,... | collective-permute-start | bytes 196616 | tf_op jit(solution)/shard_map/z_2_0/ppermute | solution.py:20
  4.1 6.2 %collective-permute-start.1 = (f32[64,256]{1,0:T(8,128)S(1)}, f32[64,256]{1,0:T(8,128)S(1)}, u32[]{:S(2)}, u32[]{:S(2)}) collective-permute-start(f32[64,256]{1,0:T(8,128)S(1)} %slice_bitcast_fusion.2), channel_id=1, source_target_pairs={{0,8},{1,9},{8,0},{9,1},{16,24},{17,25},{24,16},{25,17},{2,10},{3,... | collective-permute-start | bytes 196616 | tf_op jit(solution)/shard_map/z_1_0/ppermute | solution.py:20
  4.2 8.3 %collective-permute-start.2 = (f32[64,256]{1,0:T(8,128)S(1)}, f32[64,256]{1,0:T(8,128)S(1)}, u32[]{:S(2)}, u32[]{:S(2)}) collective-permute-start(f32[64,256]{1,0:T(8,128)S(1)} %slice_bitcast_fusion.2), channel_id=1, source_target_pairs={{0,24},{1,25},{8,16},{9,17},{16,8},{17,9},{24,0},{25,1},{2,26},{3,... | collective-permute-start | bytes 196616 | tf_op jit(solution)/shard_map/z_3_0/ppermute | solution.py:20
  5.6 9.2 %collective-permute-start.9 = (f32[2,64,256]{2,1,0:T(8,128)S(1)}, f32[2,64,256]{2,1,0:T(8,128)S(1)}, u32[]{:S(2)}, u32[]{:S(2)}) collective-permute-start(f32[2,64,256]{2,1,0:T(8,128)S(1)} %slice.45), channel_id=1, source_target_pairs={{0,16},{1,17},{8,24},{9,25},{16,0},{17,1},{24,8},{25,9},{2,18},{3,... | collective-permute-start | bytes 393224 | tf_op jit(solution)/shard_map/z_far_12/ppermute | solution.py:20
  12.5 6.5 %collective-permute-start.3 = (f32[256,256]{1,0:T(8,128)S(1)}, f32[256,256]{1,0:T(8,128)S(1)}, u32[]{:S(2)}, u32[]{:S(2)}) collective-permute-start(f32[256,256]{1,0:T(8,128)S(1)} %pad_maximum_fusion.1), channel_id=1, source_target_pairs={{0,2},{1,7},{2,0},{3,5},{4,6},{5,3},{6,4},{7,1},{8,10},{9,15},{10,... | collective-permute-start | bytes 786440 | tf_op jit(solution)/shard_map/y_first_0/ppermute | solution.py:20
  14.9 8.6 %collective-permute-start.10 = (f32[2,128,256]{2,1,0:T(8,128)S(1)}, f32[2,128,256]{2,1,0:T(8,128)S(1)}, u32[]{:S(2)}, u32[]{:S(2)}) collective-permute-start(f32[2,128,256]{2,1,0:T(8,128)S(1)} %pad_maximum_fusion.2), channel_id=1, source_target_pairs={{0,8},{1,9},{8,0},{9,1},{16,24},{17,25},{24,16},{25,17},{2,10},{3,... | collective-permute-start | bytes 786440 | tf_op jit(solution)/shard_map/z_near_12/ppermute | solution.py:20
  19.0 13.2 %collective-permute-start.4 = (f32[512,256]{1,0:T(8,128)S(1)}, f32[512,256]{1,0:T(8,128)S(1)}, u32[]{:S(2)}, u32[]{:S(2)}) collective-permute-start(f32[512,256]{1,0:T(8,128)S(1)} %constant_dynamic-update-slice_fusion.near), channel_id=1, source_target_pairs={{0,6},{1,3},{2,4},{3,1},{4,2},{5,7},{6,0},{7,5},{8,14},{9,11},{10,... | collective-permute-start | bytes 1572872 | tf_op jit(solution)/shard_map/y_second_0/ppermute | solution.py:20
  23.5 9.3 %collective-permute-start.11 = (f32[2,256,256]{2,1,0:T(8,128)S(1)}, f32[2,256,256]{2,1,0:T(8,128)S(1)}, u32[]{:S(2)}, u32[]{:S(2)}) collective-permute-start(f32[2,256,256]{2,1,0:T(8,128)S(1)} %pad_maximum_fusion), channel_id=1, source_target_pairs={{0,2},{1,7},{2,0},{3,5},{4,6},{5,3},{6,4},{7,1},{8,10},{9,15},{10,... | collective-permute-start | bytes 1572872 | tf_op jit(solution)/shard_map/y_first_12/ppermute | solution.py:20
  26.0 10.0 %collective-permute-start.5 = (f32[512,256]{1,0:T(8,128)S(1)}, f32[512,256]{1,0:T(8,128)S(1)}, u32[]{:S(2)}, u32[]{:S(2)}) collective-permute-start(f32[512,256]{1,0:T(8,128)S(1)} %constant_dynamic-update-slice_fusion.near), channel_id=1, source_target_pairs={{0,1},{1,0},{2,3},{3,2},{4,5},{5,4},{6,7},{7,6},{8,9},{9,8},{10,11... | collective-permute-start | bytes 1572872 | tf_op jit(solution)/shard_map/core_near_0/ppermute | solution.py:25
  32.2 3.9 %collective-permute-start.6 = (f32[512,256]{1,0:T(8,128)S(1)}, f32[512,256]{1,0:T(8,128)S(1)}, u32[]{:S(2)}, u32[]{:S(2)}) collective-permute-start(f32[512,256]{1,0:T(8,128)S(1)} %collective-permute-done.4.far), channel_id=1, source_target_pairs={{0,1},{1,0},{2,3},{3,2},{4,5},{5,4},{6,7},{7,6},{8,9},{9,8},{10,11... | collective-permute-start | bytes 1572872 | tf_op jit(solution)/shard_map/core_far_0/ppermute | solution.py:25
  32.9 12.3 %collective-permute-start.14 = (f32[512,256]{1,0:T(8,128)S(1)}, f32[512,256]{1,0:T(8,128)S(1)}, u32[]{:S(2)}, u32[]{:S(2)}) collective-permute-start(f32[512,256]{1,0:T(8,128)S(1)} %get-tuple-element.35.near), channel_id=1, source_target_pairs={{0,6},{1,3},{2,4},{3,1},{4,2},{5,7},{6,0},{7,5},{8,14},{9,11},{10,... | collective-permute-start | bytes 1572872 | tf_op jit(solution)/shard_map/y_second_1/ppermute | solution.py:20
  38.7 6.5 %collective-permute-start.7 = (f32[256,256]{1,0:T(8,128)S(1)}, f32[256,256]{1,0:T(8,128)S(1)}, u32[]{:S(2)}, u32[]{:S(2)}) collective-permute-start(f32[256,256]{1,0:T(8,128)S(1)} %get-tuple-element.25), channel_id=1, source_target_pairs={{0,32},{1,97},{32,0},{33,65},{64,96},{65,33},{96,64},{97,1},{2,34}... | collective-permute-start | bytes 786440 | tf_op jit(solution)/shard_map/x_first_0/ppermute | solution.py:20
  40.3 7.2 %collective-permute-start.15 = (f32[512,256]{1,0:T(8,128)S(1)}, f32[512,256]{1,0:T(8,128)S(1)}, u32[]{:S(2)}, u32[]{:S(2)}) collective-permute-start(f32[512,256]{1,0:T(8,128)S(1)} %get-tuple-element.35.near), channel_id=1, source_target_pairs={{0,1},{1,0},{2,3},{3,2},{4,5},{5,4},{6,7},{7,6},{8,9},{9,8},{10,11... | collective-permute-start | bytes 1572872 | tf_op jit(solution)/shard_map/core_near_1/ppermute | solution.py:25
  45.2 2.3 %collective-permute-start.16 = (f32[512,256]{1,0:T(8,128)S(1)}, f32[512,256]{1,0:T(8,128)S(1)}, u32[]{:S(2)}, u32[]{:S(2)}) collective-permute-start(f32[512,256]{1,0:T(8,128)S(1)} %collective-permute-done.14.far), channel_id=1, source_target_pairs={{0,1},{1,0},{2,3},{3,2},{4,5},{5,4},{6,7},{7,6},{8,9},{9,8},{10,11... | collective-permute-start | bytes 1572872 | tf_op jit(solution)/shard_map/core_far_1/ppermute | solution.py:25
  45.3 10.5 %collective-permute-start.12 = (f32[512,256]{1,0:T(8,128)S(1)}, f32[512,256]{1,0:T(8,128)S(1)}, u32[]{:S(2)}, u32[]{:S(2)}) collective-permute-start(f32[512,256]{1,0:T(8,128)S(1)} %get-tuple-element.36.near), channel_id=1, source_target_pairs={{0,6},{1,3},{2,4},{3,1},{4,2},{5,7},{6,0},{7,5},{8,14},{9,11},{10,... | collective-permute-start | bytes 1572872 | tf_op jit(solution)/shard_map/y_second_2/ppermute | solution.py:20
  47.5 12.0 %collective-permute-start.13 = (f32[512,256]{1,0:T(8,128)S(1)}, f32[512,256]{1,0:T(8,128)S(1)}, u32[]{:S(2)}, u32[]{:S(2)}) collective-permute-start(f32[512,256]{1,0:T(8,128)S(1)} %get-tuple-element.36.near), channel_id=1, source_target_pairs={{0,1},{1,0},{2,3},{3,2},{4,5},{5,4},{6,7},{7,6},{8,9},{9,8},{10,11... | collective-permute-start | bytes 1572872 | tf_op jit(solution)/shard_map/core_near_2/ppermute | solution.py:25
  55.8 3.7 %collective-permute-start.17 = (f32[512,256]{1,0:T(8,128)S(1)}, f32[512,256]{1,0:T(8,128)S(1)}, u32[]{:S(2)}, u32[]{:S(2)}) collective-permute-start(f32[512,256]{1,0:T(8,128)S(1)} %collective-permute-done.12.far), channel_id=1, source_target_pairs={{0,1},{1,0},{2,3},{3,2},{4,5},{5,4},{6,7},{7,6},{8,9},{9,8},{10,11... | collective-permute-start | bytes 1572872 | tf_op jit(solution)/shard_map/core_far_2/ppermute | solution.py:25
  55.8 7.1 %collective-permute-start.18 = (f32[256,256]{1,0:T(8,128)S(1)}, f32[256,256]{1,0:T(8,128)S(1)}, u32[]{:S(2)}, u32[]{:S(2)}) collective-permute-start(f32[256,256]{1,0:T(8,128)S(1)} %get-tuple-element.29), channel_id=1, source_target_pairs={{0,32},{1,97},{32,0},{33,65},{64,96},{65,33},{96,64},{97,1},{2,34}... | collective-permute-start | bytes 786440 | tf_op jit(solution)/shard_map/x_first_1/ppermute | solution.py:20
  57.3 9.0 %collective-permute-start.8 = (f32[128,256]{1,0:T(8,128)S(1)}, f32[128,256]{1,0:T(8,128)S(1)}, u32[]{:S(2)}, u32[]{:S(2)}) collective-permute-start(f32[128,256]{1,0:T(8,128)S(1)} %slice.57), channel_id=1, source_target_pairs={{0,96},{1,33},{32,64},{33,1},{64,32},{65,97},{96,0},{97,65},{2,98}... | collective-permute-start | bytes 393224 | tf_op jit(solution)/shard_map/x_second_0/ppermute | solution.py:20
  62.2 7.9 %collective-permute-start.21 = (f32[256,256]{1,0:T(8,128)S(1)}, f32[256,256]{1,0:T(8,128)S(1)}, u32[]{:S(2)}, u32[]{:S(2)}) collective-permute-start(f32[256,256]{1,0:T(8,128)S(1)} %get-tuple-element.32), channel_id=1, source_target_pairs={{0,32},{1,97},{32,0},{33,65},{64,96},{65,33},{96,64},{97,1},{2,34}... | collective-permute-start | bytes 786440 | tf_op jit(solution)/shard_map/x_first_2/ppermute | solution.py:20
  62.9 7.3 %collective-permute-start.19 = (f32[128,256]{1,0:T(8,128)S(1)}, f32[128,256]{1,0:T(8,128)S(1)}, u32[]{:S(2)}, u32[]{:S(2)}) collective-permute-start(f32[128,256]{1,0:T(8,128)S(1)} %slice.49), channel_id=1, source_target_pairs={{0,96},{1,33},{32,64},{33,1},{64,32},{65,97},{96,0},{97,65},{2,98}... | collective-permute-start | bytes 393224 | tf_op jit(solution)/shard_map/x_second_1/ppermute | solution.py:20
  70.1 7.7 %collective-permute-start.22 = (f32[128,256]{1,0:T(8,128)S(1)}, f32[128,256]{1,0:T(8,128)S(1)}, u32[]{:S(2)}, u32[]{:S(2)}) collective-permute-start(f32[128,256]{1,0:T(8,128)S(1)} %slice.63), channel_id=1, source_target_pairs={{0,96},{1,33},{32,64},{33,1},{64,32},{65,97},{96,0},{97,65},{2,98}... | collective-permute-start | bytes 393224 | tf_op jit(solution)/shard_map/x_second_2/ppermute | solution.py:20
  70.2 14.0 %collective-permute-start.20 = (f32[2,64,256]{2,1,0:T(8,128)S(1)}, f32[2,64,256]{2,1,0:T(8,128)S(1)}, u32[]{:S(2)}, u32[]{:S(2)}) collective-permute-start(f32[2,64,256]{2,1,0:T(8,128)S(1)} %pad_maximum_fusion.4), channel_id=1, source_target_pairs={{0,128},{1,129},{128,0},{129,1},{2,130},{3,131},{130,2},{131,3},{4... | collective-permute-start | bytes 393224 | tf_op jit(solution)/shard_map/zh_01/ppermute | solution.py:20
  77.8 8.6 %collective-permute-start.23 = (f32[64,256]{1,0:T(8,128)S(1)}, f32[64,256]{1,0:T(8,128)S(1)}, u32[]{:S(2)}, u32[]{:S(2)}) collective-permute-start(f32[64,256]{1,0:T(8,128)S(1)} %slice.65), channel_id=1, source_target_pairs={{0,128},{1,129},{128,0},{129,1},{2,130},{3,131},{130,2},{131,3},{4... | collective-permute-start | bytes 196616 | tf_op jit(solution)/shard_map/zh_2/ppermute | solution.py:20

commit v2 on v1

--- a/solution.py
+++ b/solution.py
@@ -130,8 +130,10 @@
     near_z, far_z, first, second, across = (1, 1), (2, 2), (1, 3), (3, 1), (1, 1)
 
     own = lower_panel[0]
-    g0 = jnp.concatenate([own] + [swap(own, "zl", (dz, dz), "z_{}_0".format(dz)) for dz in (2, 1, 3)])
-    a12 = grow(lower_panel[1:], "zl", far_z, "z_far_12")
+    far = swap(lower_panel, "zl", far_z, "z_far")
+    z1, z3 = swap(own, "zl", (1, 1), "z_1_0"), swap(own, "zl", (3, 3), "z_3_0")
+    g0 = jnp.concatenate([own, far[0], z1, z3])
+    a12 = jnp.concatenate([lower_panel[1:], far[1:]], axis=1)
     g12 = grow(a12, "zl", near_z, "z_near_12")
     n0 = grow(g0, "y", first, "y_first_0")
     high, low = split_tiles(spot, inverse_tiles, after(factors, n0))

time: 87.8 us -> 92.8 us (1.057)
  waiting for transfers between devices: 23.2 us -> 38.7 us
  starting transfers between devices: 45.6 us -> 35.5 us
    ppermute x18 -> x17, waiting for transfers between devices: 23.2 us -> 38.6 us  [swap(): return lax.ppermute(value, (axis, 'core'), pairs)]
    ppermute x18 -> x17, starting transfers between devices: 44.7 us -> 35.4 us  [swap(): return lax.ppermute(value, (axis, 'core'), pairs)]
  transfers between devices with their start and end apart: 24 -> 23, of which waited for: 10 -> 9; matrix products, arithmetic and copies ran while one was open for 4% -> 3% of each run, Pallas kernels for 15% -> 15%
where the time goes in v2:
time: 92.8 us; the launch traced here: 92.6 us
  waiting for transfers between devices  38.7 us (42%)
  starting transfers between devices  35.5 us (38%)
  Pallas kernels  13.4 us (14%)
  local copies, waits for them, and re-layouts  3.03 us (3%)
  other arithmetic  1.66 us (2%)
    ppermute x17, waiting for transfers between devices, swap(): return lax.ppermute(value, (axis, 'core'), pairs)  38.6 us
    ppermute x17, starting transfers between devices, swap(): return lax.ppermute(value, (axis, 'core'), pairs)  35.4 us
    pallas_call x3, Pallas kernels, product(): pl.pallas_call(functools.partial(product_kernel, n), out_shape=[jax.Shape...  7.99 us
    pallas_call x1, Pallas kernels, split_tiles(): pl.pallas_call(tiles_kernel, out_shape=[out, out], in_specs=[pl.BlockSpec...  5.45 us
  transfers between devices with their start and end apart: 23, of which 9 were waited for; matrix products, arithmetic and copies ran while one was open for 3% of the time, Pallas kernels for 15%

profile of v2, /device:TPU:32, one launch (start us, length us, event | category | flops | bytes accessed | tf_op | source)
XLA Modules:
  0.0 92.6 jit_solution(12440408968785098007)
XLA Ops:
  0.0 0.8 slice_bitcast_fusion.3
  0.8 1.8 %collective-permute-start.1 = (f32[64,256]{1,0:T(8,128)S(1)}, f32[64,256]{1,0:T(8,128)S(1)}, u32[]{:S(2)}, u32[]{:S(2)}) collective-permute-start(f32[64,256]{1,0:T(8,128)S(1)} %slice_bitcast_fusion.3), channel_id=1, source_target_pairs={{0,8},{1,9},{8,0},{9,1},{16,24},{17,25},{24,16},{25,17},{2,10},{3,... | collective-permute-start | bytes 196616 | tf_op jit(solution)/shard_map/z_1_0/ppermute | solution.py:20
  2.7 2.0 %collective-permute-start.2 = (f32[64,256]{1,0:T(8,128)S(1)}, f32[64,256]{1,0:T(8,128)S(1)}, u32[]{:S(2)}, u32[]{:S(2)}) collective-permute-start(f32[64,256]{1,0:T(8,128)S(1)} %slice_bitcast_fusion.3), channel_id=1, source_target_pairs={{0,24},{1,25},{8,16},{9,17},{16,8},{17,9},{24,0},{25,1},{2,26},{3,... | collective-permute-start | bytes 196616 | tf_op jit(solution)/shard_map/z_3_0/ppermute | solution.py:20
  4.7 0.6 collective-permute-start
  5.2 0.9 %slice.52 = f32[2,64,256]{2,1,0:T(8,128)S(1)} slice(f32[3,64,256]{2,1,0:T(8,128)} %param.4), slice={[1:3], [0:64], [0:256]} | slice | bytes 262144 | tf_op jit(solution)/shard_map/slice | solution.py:136
  6.2 0.8 constant_dynamic-update-slice_fusion.4
  7.0 8.7 %collective-permute-done = f32[3,64,256]{2,1,0:T(8,128)S(1)} collective-permute-done((f32[3,64,256]{2,1,0:T(8,128)}, f32[3,64,256]{2,1,0:T(8,128)S(1)}, u32[]{:S(2)}, u32[]{:S(2)}) %collective-permute-start) | collective-permute-done | bytes 196640 | tf_op jit(solution)/shard_map/z_far/ppermute | solution.py:20
  15.7 0.0 collective-permute-done.1
  15.7 1.7 %collective-permute-start.3 = (f32[256,256]{1,0:T(8,128)S(1)}, f32[256,256]{1,0:T(8,128)S(1)}, u32[]{:S(2)}, u32[]{:S(2)}) collective-permute-start(f32[256,256]{1,0:T(8,128)S(1)} %pad_maximum_fusion.1), channel_id=1, source_target_pairs={{0,2},{1,7},{2,0},{3,5},{4,6},{5,3},{6,4},{7,1},{8,10},{9,15},{10,... | collective-permute-start | bytes 786440 | tf_op jit(solution)/shard_map/y_first_0/ppermute | solution.py:20
  17.4 2.2 %collective-permute-start.9 = (f32[2,128,256]{2,1,0:T(8,128)S(1)}, f32[2,128,256]{2,1,0:T(8,128)S(1)}, u32[]{:S(2)}, u32[]{:S(2)}) collective-permute-start(f32[2,128,256]{2,1,0:T(8,128)S(1)} %pad_maximum_fusion.2), channel_id=1, source_target_pairs={{0,8},{1,9},{8,0},{9,1},{16,24},{17,25},{24,16},{25,17},{2,10},{3,... | collective-permute-start | bytes 786440 | tf_op jit(solution)/shard_map/z_near_12/ppermute | solution.py:20
  19.7 2.5 %collective-permute-done.3 = f32[256,256]{1,0:T(8,128)S(1)} collective-permute-done((f32[256,256]{1,0:T(8,128)S(1)}, f32[256,256]{1,0:T(8,128)S(1)}, u32[]{:S(2)}, u32[]{:S(2)}) %collective-permute-start.3) | collective-permute-done | bytes 262176 | tf_op jit(solution)/shard_map/y_first_0/ppermute | solution.py:20
  22.2 3.1 %collective-permute-start.4 = (f32[512,256]{1,0:T(8,128)S(1)}, f32[512,256]{1,0:T(8,128)S(1)}, u32[]{:S(2)}, u32[]{:S(2)}) collective-permute-start(f32[512,256]{1,0:T(8,128)S(1)} %constant_dynamic-update-slice_fusion.near), channel_id=1, source_target_pairs={{0,6},{1,3},{2,4},{3,1},{4,2},{5,7},{6,0},{7,5},{8,14},{9,11},{10,... | collective-permute-start | bytes 1572872 | tf_op jit(solution)/shard_map/y_second_0/ppermute | solution.py:20
  25.3 1.2 %collective-permute-done.9 = f32[2,128,256]{2,1,0:T(8,128)S(1)} collective-permute-done((f32[2,128,256]{2,1,0:T(8,128)S(1)}, f32[2,128,256]{2,1,0:T(8,128)S(1)}, u32[]{:S(2)}, u32[]{:S(2)}) %collective-permute-start.9) | collective-permute-done | bytes 262176 | tf_op jit(solution)/shard_map/z_near_12/ppermute | solution.py:20
  26.6 0.8 collective-permute-start.10
  27.3 0.1 stack.32.spot
  27.4 0.7 convert_negate_fusion
  28.1 0.0 collective-permute-start.5
  28.1 0.1 broadcast_in_dim.7
  28.2 5.5 %split_tiles.1 = (bf16[3,512,2048]{2,1,0:T(8,128)(2,1)S(1)}, bf16[3,512,2048]{2,1,0:T(8,128)(2,1)S(1)}) custom-call(s32[5]{0:T(128)S(1)} %stack.32.spot, f32[3,4,1,2048]{3,2,1,0:T(1,128)S(1)} %bitcast.23, f32[3,512,2048]{2,1,0:T(8,128)} %tiles.1), custom_call_target="tpu_custom_call" | custom-call | tf_op jit(solution)/shard_map/split_tiles/pallas_call | solution.py:65
  33.7 3.2 %collective-permute-done.4.far = f32[512,256]{1,0:T(8,128)S(1)} collective-permute-done((f32[512,256]{1,0:T(8,128)S(1)}, f32[512,256]{1,0:T(8,128)S(1)}, u32[]{:S(2)}, u32[]{:S(2)}) %collective-permute-start.4) | collective-permute-done | bytes 524320 | tf_op jit(solution)/shard_map/y_second_0/ppermute | solution.py:20
  36.9 0.0 collective-permute-start.6
  36.9 0.0 collective-permute-done.10
  37.0 0.1 slice_bitcast_fusion
  37.1 3.8 %collective-permute-start.13 = (f32[512,256]{1,0:T(8,128)S(1)}, f32[512,256]{1,0:T(8,128)S(1)}, u32[]{:S(2)}, u32[]{:S(2)}) collective-permute-start(f32[512,256]{1,0:T(8,128)S(1)} %get-tuple-element.35.near), channel_id=1, source_target_pairs={{0,6},{1,3},{2,4},{3,1},{4,2},{5,7},{6,0},{7,5},{8,14},{9,11},{10,... | collective-permute-start | bytes 1572872 | tf_op jit(solution)/shard_map/y_second_1/ppermute | solution.py:20
  40.8 2.7 %product.3 = (f32[256,256]{1,0:T(8,128)S(1)}, f32[256,256]{1,0:T(8,128)S(1)}) custom-call(s32[5]{0:T(128)S(1)} %stack.32.spot, bf16[3,512,2048]{2,1,0:T(8,128)(2,1)S(1)} %get-tuple-element.21.high, bf16[3,512,2048]{2,1,0:T(8,128)(2,1)S(1)} %get-tuple-element.22.low, f32[512,256]{1,0:T(8,128)S(1)} %constant_dynamic-update-slice_fusion.near, ...), custom_call_target="tpu_custom_call" | custom-call | tf_op jit(solution)/shard_map/product/pallas_call | solution.py:100
  43.5 1.6 %collective-permute-start.7 = (f32[256,256]{1,0:T(8,128)S(1)}, f32[256,256]{1,0:T(8,128)S(1)}, u32[]{:S(2)}, u32[]{:S(2)}) collective-permute-start(f32[256,256]{1,0:T(8,128)S(1)} %get-tuple-element.25), channel_id=1, source_target_pairs={{0,32},{1,97},{32,0},{33,65},{64,96},{65,33},{96,64},{97,1},{2,34}... | collective-permute-start | bytes 786440 | tf_op jit(solution)/shard_map/x_first_0/ppermute | solution.py:20
  45.1 4.9 %collective-permute-done.7 = f32[256,256]{1,0:T(8,128)S(1)} collective-permute-done((f32[256,256]{1,0:T(8,128)S(1)}, f32[256,256]{1,0:T(8,128)S(1)}, u32[]{:S(2)}, u32[]{:S(2)}) %collective-permute-start.7) | collective-permute-done | bytes 262176 | tf_op jit(solution)/shard_map/x_first_0/ppermute | solution.py:20
  50.0 0.0 collective-permute-done.13.far
  50.0 0.1 collective-permute-start.15
  50.1 1.9 %collective-permute-start.11 = (f32[512,256]{1,0:T(8,128)S(1)}, f32[512,256]{1,0:T(8,128)S(1)}, u32[]{:S(2)}, u32[]{:S(2)}) collective-permute-start(f32[512,256]{1,0:T(8,128)S(1)} %get-tuple-element.36.near), channel_id=1, source_target_pairs={{0,6},{1,3},{2,4},{3,1},{4,2},{5,7},{6,0},{7,5},{8,14},{9,11},{10,... | collective-permute-start | bytes 1572872 | tf_op jit(solution)/shard_map/y_second_2/ppermute | solution.py:20
  52.0 0.0 collective-permute-start.12
  52.0 2.7 %product.4 = (f32[256,256]{1,0:T(8,128)S(1)}, f32[256,256]{1,0:T(8,128)S(1)}) custom-call(s32[5]{0:T(128)S(1)} %stack.32.spot, bf16[3,512,2048]{2,1,0:T(8,128)(2,1)S(1)} %get-tuple-element.21.high, bf16[3,512,2048]{2,1,0:T(8,128)(2,1)S(1)} %get-tuple-element.22.low, f32[512,256]{1,0:T(8,128)S(1)} %get-tuple-element.35.near, ...), custom_call_target="tpu_custom_call" | custom-call | tf_op jit(solution)/shard_map/product/pallas_call | solution.py:100
  54.7 5.9 %collective-permute-done.11.far = f32[512,256]{1,0:T(8,128)S(1)} collective-permute-done((f32[512,256]{1,0:T(8,128)S(1)}, f32[512,256]{1,0:T(8,128)S(1)}, u32[]{:S(2)}, u32[]{:S(2)}) %collective-permute-start.11) | collective-permute-done | bytes 524320 | tf_op jit(solution)/shard_map/y_second_2/ppermute | solution.py:20
  60.6 0.0 collective-permute-start.16
  60.6 1.5 %collective-permute-start.17 = (f32[256,256]{1,0:T(8,128)S(1)}, f32[256,256]{1,0:T(8,128)S(1)}, u32[]{:S(2)}, u32[]{:S(2)}) collective-permute-start(f32[256,256]{1,0:T(8,128)S(1)} %get-tuple-element.29), channel_id=1, source_target_pairs={{0,32},{1,97},{32,0},{33,65},{64,96},{65,33},{96,64},{97,1},{2,34}... | collective-permute-start | bytes 786440 | tf_op jit(solution)/shard_map/x_first_1/ppermute | solution.py:20
  62.1 2.2 %collective-permute-start.8 = (f32[128,256]{1,0:T(8,128)S(1)}, f32[128,256]{1,0:T(8,128)S(1)}, u32[]{:S(2)}, u32[]{:S(2)}) collective-permute-start(f32[128,256]{1,0:T(8,128)S(1)} %slice.66), channel_id=1, source_target_pairs={{0,96},{1,33},{32,64},{33,1},{64,32},{65,97},{96,0},{97,65},{2,98}... | collective-permute-start | bytes 393224 | tf_op jit(solution)/shard_map/x_second_0/ppermute | solution.py:20
  64.3 0.0 collective-permute-done.12.near_other
  64.3 0.0 collective-permute-done.16.far_other
  64.3 2.7 %product.5 = (f32[256,256]{1,0:T(8,128)S(1)}, f32[256,256]{1,0:T(8,128)S(1)}) custom-call(s32[5]{0:T(128)S(1)} %stack.32.spot, bf16[3,512,2048]{2,1,0:T(8,128)(2,1)S(1)} %get-tuple-element.21.high, bf16[3,512,2048]{2,1,0:T(8,128)(2,1)S(1)} %get-tuple-element.22.low, f32[512,256]{1,0:T(8,128)S(1)} %get-tuple-element.36.near, ...), custom_call_target="tpu_custom_call" | custom-call | tf_op jit(solution)/shard_map/product/pallas_call | solution.py:100
  67.0 0.7 collective-permute-start.20
  67.7 3.4 %collective-permute-start.18 = (f32[128,256]{1,0:T(8,128)S(1)}, f32[128,256]{1,0:T(8,128)S(1)}, u32[]{:S(2)}, u32[]{:S(2)}) collective-permute-start(f32[128,256]{1,0:T(8,128)S(1)} %slice.57), channel_id=1, source_target_pairs={{0,96},{1,33},{32,64},{33,1},{64,32},{65,97},{96,0},{97,65},{2,98}... | collective-permute-start | bytes 393224 | tf_op jit(solution)/shard_map/x_second_1/ppermute | solution.py:20
  71.1 3.7 %collective-permute-done.20 = f32[256,256]{1,0:T(8,128)S(1)} collective-permute-done((f32[256,256]{1,0:T(8,128)S(1)}, f32[256,256]{1,0:T(8,128)S(1)}, u32[]{:S(2)}, u32[]{:S(2)}) %collective-permute-start.20) | collective-permute-done | bytes 262176 | tf_op jit(solution)/shard_map/x_first_2/ppermute | solution.py:20
  74.9 0.1 collective-permute-start.21
  75.0 4.1 %collective-permute-start.19 = (f32[2,64,256]{2,1,0:T(8,128)S(1)}, f32[2,64,256]{2,1,0:T(8,128)S(1)}, u32[]{:S(2)}, u32[]{:S(2)}) collective-permute-start(f32[2,64,256]{2,1,0:T(8,128)S(1)} %pad_maximum_fusion.4), channel_id=1, source_target_pairs={{0,128},{1,129},{128,0},{129,1},{2,130},{3,131},{130,2},{131,3},{4... | collective-permute-start | bytes 393224 | tf_op jit(solution)/shard_map/zh_01/ppermute | solution.py:20
  79.1 2.0 %collective-permute-done.21 = f32[128,256]{1,0:T(8,128)S(1)} collective-permute-done((f32[128,256]{1,0:T(8,128)S(1)}, f32[128,256]{1,0:T(8,128)S(1)}, u32[]{:S(2)}, u32[]{:S(2)}) %collective-permute-start.21) | collective-permute-done | bytes 131104 | tf_op jit(solution)/shard_map/x_second_2/ppermute | solution.py:20
  81.2 4.1 %collective-permute-start.22 = (f32[64,256]{1,0:T(8,128)S(1)}, f32[64,256]{1,0:T(8,128)S(1)}, u32[]{:S(2)}, u32[]{:S(2)}) collective-permute-start(f32[64,256]{1,0:T(8,128)S(1)} %slice.75), channel_id=1, source_target_pairs={{0,128},{1,129},{128,0},{129,1},{2,130},{3,131},{130,2},{131,3},{4... | collective-permute-start | bytes 196616 | tf_op jit(solution)/shard_map/zh_2/ppermute | solution.py:20
  85.3 6.5 %collective-permute-done.22 = f32[64,256]{1,0:T(8,128)S(1)} collective-permute-done((f32[64,256]{1,0:T(8,128)S(1)}, f32[64,256]{1,0:T(8,128)S(1)}, u32[]{:S(2)}, u32[]{:S(2)}) %collective-permute-start.22) | collective-permute-done | bytes 65568 | tf_op jit(solution)/shard_map/zh_2/ppermute | solution.py:20
  91.9 0.7 pad_maximum_fusion.3
  (34 shorter events, 0.4 us)
Async XLA Ops:
  0.8 14.9 %collective-permute-start.1 = (f32[64,256]{1,0:T(8,128)S(1)}, f32[64,256]{1,0:T(8,128)S(1)}, u32[]{:S(2)}, u32[]{:S(2)}) collective-permute-start(f32[64,256]{1,0:T(8,128)S(1)} %slice_bitcast_fusion.3), channel_id=1, source_target_pairs={{0,8},{1,9},{8,0},{9,1},{16,24},{17,25},{24,16},{25,17},{2,10},{3,... | collective-permute-start | bytes 196616 | tf_op jit(solution)/shard_map/z_1_0/ppermute | solution.py:20
  2.7 13.0 %collective-permute-start.2 = (f32[64,256]{1,0:T(8,128)S(1)}, f32[64,256]{1,0:T(8,128)S(1)}, u32[]{:S(2)}, u32[]{:S(2)}) collective-permute-start(f32[64,256]{1,0:T(8,128)S(1)} %slice_bitcast_fusion.3), channel_id=1, source_target_pairs={{0,24},{1,25},{8,16},{9,17},{16,8},{17,9},{24,0},{25,1},{2,26},{3,... | collective-permute-start | bytes 196616 | tf_op jit(solution)/shard_map/z_3_0/ppermute | solution.py:20
  4.7 11.0 %collective-permute-start = (f32[3,64,256]{2,1,0:T(8,128)}, f32[3,64,256]{2,1,0:T(8,128)S(1)}, u32[]{:S(2)}, u32[]{:S(2)}) collective-permute-start(f32[3,64,256]{2,1,0:T(8,128)} %param.4), channel_id=1, source_target_pairs={{0,16},{1,17},{8,24},{9,25},{16,0},{17,1},{24,8},{25,9},{2,18},{3,... | collective-permute-start | bytes 589832 | tf_op jit(solution)/shard_map/z_far/ppermute | solution.py:20
  15.7 6.5 %collective-permute-start.3 = (f32[256,256]{1,0:T(8,128)S(1)}, f32[256,256]{1,0:T(8,128)S(1)}, u32[]{:S(2)}, u32[]{:S(2)}) collective-permute-start(f32[256,256]{1,0:T(8,128)S(1)} %pad_maximum_fusion.1), channel_id=1, source_target_pairs={{0,2},{1,7},{2,0},{3,5},{4,6},{5,3},{6,4},{7,1},{8,10},{9,15},{10,... | collective-permute-start | bytes 786440 | tf_op jit(solution)/shard_map/y_first_0/ppermute | solution.py:20
  17.4 9.1 %collective-permute-start.9 = (f32[2,128,256]{2,1,0:T(8,128)S(1)}, f32[2,128,256]{2,1,0:T(8,128)S(1)}, u32[]{:S(2)}, u32[]{:S(2)}) collective-permute-start(f32[2,128,256]{2,1,0:T(8,128)S(1)} %pad_maximum_fusion.2), channel_id=1, source_target_pairs={{0,8},{1,9},{8,0},{9,1},{16,24},{17,25},{24,16},{25,17},{2,10},{3,... | collective-permute-start | bytes 786440 | tf_op jit(solution)/shard_map/z_near_12/ppermute | solution.py:20
  22.2 14.7 %collective-permute-start.4 = (f32[512,256]{1,0:T(8,128)S(1)}, f32[512,256]{1,0:T(8,128)S(1)}, u32[]{:S(2)}, u32[]{:S(2)}) collective-permute-start(f32[512,256]{1,0:T(8,128)S(1)} %constant_dynamic-update-slice_fusion.near), channel_id=1, source_target_pairs={{0,6},{1,3},{2,4},{3,1},{4,2},{5,7},{6,0},{7,5},{8,14},{9,11},{10,... | collective-permute-start | bytes 1572872 | tf_op jit(solution)/shard_map/y_second_0/ppermute | solution.py:20
  26.6 10.4 %collective-permute-start.10 = (f32[2,256,256]{2,1,0:T(8,128)S(1)}, f32[2,256,256]{2,1,0:T(8,128)S(1)}, u32[]{:S(2)}, u32[]{:S(2)}) collective-permute-start(f32[2,256,256]{2,1,0:T(8,128)S(1)} %pad_maximum_fusion), channel_id=1, source_target_pairs={{0,2},{1,7},{2,0},{3,5},{4,6},{5,3},{6,4},{7,1},{8,10},{9,15},{10,... | collective-permute-start | bytes 1572872 | tf_op jit(solution)/shard_map/y_first_12/ppermute | solution.py:20
  28.1 12.7 %collective-permute-start.5 = (f32[512,256]{1,0:T(8,128)S(1)}, f32[512,256]{1,0:T(8,128)S(1)}, u32[]{:S(2)}, u32[]{:S(2)}) collective-permute-start(f32[512,256]{1,0:T(8,128)S(1)} %constant_dynamic-update-slice_fusion.near), channel_id=1, source_target_pairs={{0,1},{1,0},{2,3},{3,2},{4,5},{5,4},{6,7},{7,6},{8,9},{9,8},{10,11... | collective-permute-start | bytes 1572872 | tf_op jit(solution)/shard_map/core_near_0/ppermute | solution.py:25
  36.9 3.9 %collective-permute-start.6 = (f32[512,256]{1,0:T(8,128)S(1)}, f32[512,256]{1,0:T(8,128)S(1)}, u32[]{:S(2)}, u32[]{:S(2)}) collective-permute-start(f32[512,256]{1,0:T(8,128)S(1)} %collective-permute-done.4.far), channel_id=1, source_target_pairs={{0,1},{1,0},{2,3},{3,2},{4,5},{5,4},{6,7},{7,6},{8,9},{9,8},{10,11... | collective-permute-start | bytes 1572872 | tf_op jit(solution)/shard_map/core_far_0/ppermute | solution.py:25
  37.1 12.9 %collective-permute-start.13 = (f32[512,256]{1,0:T(8,128)S(1)}, f32[512,256]{1,0:T(8,128)S(1)}, u32[]{:S(2)}, u32[]{:S(2)}) collective-permute-start(f32[512,256]{1,0:T(8,128)S(1)} %get-tuple-element.35.near), channel_id=1, source_target_pairs={{0,6},{1,3},{2,4},{3,1},{4,2},{5,7},{6,0},{7,5},{8,14},{9,11},{10,... | collective-permute-start | bytes 1572872 | tf_op jit(solution)/shard_map/y_second_1/ppermute | solution.py:20
  43.5 6.5 %collective-permute-start.7 = (f32[256,256]{1,0:T(8,128)S(1)}, f32[256,256]{1,0:T(8,128)S(1)}, u32[]{:S(2)}, u32[]{:S(2)}) collective-permute-start(f32[256,256]{1,0:T(8,128)S(1)} %get-tuple-element.25), channel_id=1, source_target_pairs={{0,32},{1,97},{32,0},{33,65},{64,96},{65,33},{96,64},{97,1},{2,34}... | collective-permute-start | bytes 786440 | tf_op jit(solution)/shard_map/x_first_0/ppermute | solution.py:20
  45.1 6.9 %collective-permute-start.14 = (f32[512,256]{1,0:T(8,128)S(1)}, f32[512,256]{1,0:T(8,128)S(1)}, u32[]{:S(2)}, u32[]{:S(2)}) collective-permute-start(f32[512,256]{1,0:T(8,128)S(1)} %get-tuple-element.35.near), channel_id=1, source_target_pairs={{0,1},{1,0},{2,3},{3,2},{4,5},{5,4},{6,7},{7,6},{8,9},{9,8},{10,11... | collective-permute-start | bytes 1572872 | tf_op jit(solution)/shard_map/core_near_1/ppermute | solution.py:25
  50.0 2.0 %collective-permute-start.15 = (f32[512,256]{1,0:T(8,128)S(1)}, f32[512,256]{1,0:T(8,128)S(1)}, u32[]{:S(2)}, u32[]{:S(2)}) collective-permute-start(f32[512,256]{1,0:T(8,128)S(1)} %collective-permute-done.13.far), channel_id=1, source_target_pairs={{0,1},{1,0},{2,3},{3,2},{4,5},{5,4},{6,7},{7,6},{8,9},{9,8},{10,11... | collective-permute-start | bytes 1572872 | tf_op jit(solution)/shard_map/core_far_1/ppermute | solution.py:25
  50.1 10.5 %collective-permute-start.11 = (f32[512,256]{1,0:T(8,128)S(1)}, f32[512,256]{1,0:T(8,128)S(1)}, u32[]{:S(2)}, u32[]{:S(2)}) collective-permute-start(f32[512,256]{1,0:T(8,128)S(1)} %get-tuple-element.36.near), channel_id=1, source_target_pairs={{0,6},{1,3},{2,4},{3,1},{4,2},{5,7},{6,0},{7,5},{8,14},{9,11},{10,... | collective-permute-start | bytes 1572872 | tf_op jit(solution)/shard_map/y_second_2/ppermute | solution.py:20
  52.0 12.3 %collective-permute-start.12 = (f32[512,256]{1,0:T(8,128)S(1)}, f32[512,256]{1,0:T(8,128)S(1)}, u32[]{:S(2)}, u32[]{:S(2)}) collective-permute-start(f32[512,256]{1,0:T(8,128)S(1)} %get-tuple-element.36.near), channel_id=1, source_target_pairs={{0,1},{1,0},{2,3},{3,2},{4,5},{5,4},{6,7},{7,6},{8,9},{9,8},{10,11... | collective-permute-start | bytes 1572872 | tf_op jit(solution)/shard_map/core_near_2/ppermute | solution.py:25
  60.6 3.7 %collective-permute-start.16 = (f32[512,256]{1,0:T(8,128)S(1)}, f32[512,256]{1,0:T(8,128)S(1)}, u32[]{:S(2)}, u32[]{:S(2)}) collective-permute-start(f32[512,256]{1,0:T(8,128)S(1)} %collective-permute-done.11.far), channel_id=1, source_target_pairs={{0,1},{1,0},{2,3},{3,2},{4,5},{5,4},{6,7},{7,6},{8,9},{9,8},{10,11... | collective-permute-start | bytes 1572872 | tf_op jit(solution)/shard_map/core_far_2/ppermute | solution.py:25
  60.6 7.1 %collective-permute-start.17 = (f32[256,256]{1,0:T(8,128)S(1)}, f32[256,256]{1,0:T(8,128)S(1)}, u32[]{:S(2)}, u32[]{:S(2)}) collective-permute-start(f32[256,256]{1,0:T(8,128)S(1)} %get-tuple-element.29), channel_id=1, source_target_pairs={{0,32},{1,97},{32,0},{33,65},{64,96},{65,33},{96,64},{97,1},{2,34}... | collective-permute-start | bytes 786440 | tf_op jit(solution)/shard_map/x_first_1/ppermute | solution.py:20
  62.1 9.0 %collective-permute-start.8 = (f32[128,256]{1,0:T(8,128)S(1)}, f32[128,256]{1,0:T(8,128)S(1)}, u32[]{:S(2)}, u32[]{:S(2)}) collective-permute-start(f32[128,256]{1,0:T(8,128)S(1)} %slice.66), channel_id=1, source_target_pairs={{0,96},{1,33},{32,64},{33,1},{64,32},{65,97},{96,0},{97,65},{2,98}... | collective-permute-start | bytes 393224 | tf_op jit(solution)/shard_map/x_second_0/ppermute | solution.py:20
  67.0 7.9 %collective-permute-start.20 = (f32[256,256]{1,0:T(8,128)S(1)}, f32[256,256]{1,0:T(8,128)S(1)}, u32[]{:S(2)}, u32[]{:S(2)}) collective-permute-start(f32[256,256]{1,0:T(8,128)S(1)} %get-tuple-element.32), channel_id=1, source_target_pairs={{0,32},{1,97},{32,0},{33,65},{64,96},{65,33},{96,64},{97,1},{2,34}... | collective-permute-start | bytes 786440 | tf_op jit(solution)/shard_map/x_first_2/ppermute | solution.py:20
  67.7 7.3 %collective-permute-start.18 = (f32[128,256]{1,0:T(8,128)S(1)}, f32[128,256]{1,0:T(8,128)S(1)}, u32[]{:S(2)}, u32[]{:S(2)}) collective-permute-start(f32[128,256]{1,0:T(8,128)S(1)} %slice.57), channel_id=1, source_target_pairs={{0,96},{1,33},{32,64},{33,1},{64,32},{65,97},{96,0},{97,65},{2,98}... | collective-permute-start | bytes 393224 | tf_op jit(solution)/shard_map/x_second_1/ppermute | solution.py:20
  74.9 6.3 %collective-permute-start.21 = (f32[128,256]{1,0:T(8,128)S(1)}, f32[128,256]{1,0:T(8,128)S(1)}, u32[]{:S(2)}, u32[]{:S(2)}) collective-permute-start(f32[128,256]{1,0:T(8,128)S(1)} %slice.73), channel_id=1, source_target_pairs={{0,96},{1,33},{32,64},{33,1},{64,32},{65,97},{96,0},{97,65},{2,98}... | collective-permute-start | bytes 393224 | tf_op jit(solution)/shard_map/x_second_2/ppermute | solution.py:20
  75.0 10.3 %collective-permute-start.19 = (f32[2,64,256]{2,1,0:T(8,128)S(1)}, f32[2,64,256]{2,1,0:T(8,128)S(1)}, u32[]{:S(2)}, u32[]{:S(2)}) collective-permute-start(f32[2,64,256]{2,1,0:T(8,128)S(1)} %pad_maximum_fusion.4), channel_id=1, source_target_pairs={{0,128},{1,129},{128,0},{129,1},{2,130},{3,131},{130,2},{131,3},{4... | collective-permute-start | bytes 393224 | tf_op jit(solution)/shard_map/zh_01/ppermute | solution.py:20
  81.2 10.7 %collective-permute-start.22 = (f32[64,256]{1,0:T(8,128)S(1)}, f32[64,256]{1,0:T(8,128)S(1)}, u32[]{:S(2)}, u32[]{:S(2)}) collective-permute-start(f32[64,256]{1,0:T(8,128)S(1)} %slice.75), channel_id=1, source_target_pairs={{0,128},{1,129},{128,0},{129,1},{2,130},{3,131},{130,2},{131,3},{4... | collective-permute-start | bytes 196616 | tf_op jit(solution)/shard_map/zh_2/ppermute | solution.py:20
